TPU v7x, 256 devices: a whole 4x4x8 slice. The times are simulated.
256 devices in a mesh: pat: 16 (over x_lo, y, core), tile: 16 (over z, x_hi).
Axes of the slice: x: 4 (x_hi: 2, x_lo: 2; x = x_hi * 2 + x_lo), y: 4, z: 8, core: 2. Of those that a mesh axis runs over, the one named last changes fastest.
Arguments:
- patch_class_features: bfloat16 [32768, 1536], P(('pat', 'tile')), may hold values from -6 to 6
- live_tiles: int32 [256], P(('pat', 'tile')), may hold values from 32 to 128, as said below
- tile_patient: int32 [32768], P(('pat', 'tile')), may hold values from 0 to 3, as said below
- ln_gain: float32 [1536], replicated, may hold values from 0.25 to 1.75
- up_weight: bfloat16 [1536, 6144], P(None, 'tile'), may hold values from -0.15625 to 0.15625
- down_weight: bfloat16 [6144, 1536], P('tile'), may hold values from -0.078125 to 0.078125
- tanh_weight: bfloat16 [1536, 256], P('tile'), may hold values from -0.15625 to 0.15625
- sigmoid_weight: bfloat16 [1536, 256], P('tile'), may hold values from -0.15625 to 0.15625
- score_weight: float32 [256], replicated, may hold values from -0.25 to 0.25
- queue_keys: bfloat16 [16384, 1536], P('tile'), may hold values from -6 to 6
- queue_labels: int32 [16384], P('tile'), may hold values from 0 to 3, as said below
- patient_labels: int32 [64], P('pat'), may hold values from 0 to 3
- loss_scale: float32 [], replicated, may hold values from 1024 to 8192
Outputs:
- up_grad: float32 [1536, 6144], P('pat', 'tile')
- down_grad: float32 [6144, 1536], P('tile', 'pat')
- tanh_grad: float32 [1536, 256], P('tile')
- sigmoid_grad: float32 [1536, 256], P('tile')
- score_grad: float32 [256], replicated
- contrastive_loss: float32 [], replicated
Inputs may be any that keep to these rules, and one draw needn't show every extreme that they name: `live_tiles`: some device has all 128 slots live in every draw. `tile_patient`: every patient has at least one live tile. `queue_labels`: every class appears in the queue.
All inputs are finite; a program needn't handle non-finite values.
Results may differ from a plain program's by a relative error of at most 0.03.
Values may be sent and summed in bfloat16 or wider, within the bound.
A program may use at most 192 MiB of HBM per device.

v0:
```python
import jax
import jax.numpy as jnp
from jax import lax
from jax.sharding import PartitionSpec as P

sharpness_divisor = 0.07
highest = lax.Precision.HIGHEST


def layer_norm(row_block, ln_gain):
    values = row_block.astype(jnp.float32)
    center = values - jnp.mean(values, axis=1, keepdims=True)
    spread = jnp.mean(center * center, axis=1, keepdims=True)
    return (center * lax.rsqrt(spread + 1e-06) * ln_gain).astype(jnp.bfloat16)


def gelu_value(preact):
    return 0.5 * preact * (1.0 + lax.erf(preact * 0.7071067811865476))


def gelu_slope(preact):
    return (
        0.5 * (1.0 + lax.erf(preact * 0.7071067811865476))
        + preact * jnp.exp(-0.5 * preact * preact) * 0.3989422804014327
    )


def gate_backward(score_grads, tanh_val, sigmoid_val, score_weight):
    common = score_grads[:, None] * score_weight
    tanh_pre = (common * sigmoid_val * (1.0 - tanh_val * tanh_val)).astype(jnp.bfloat16)
    sigmoid_pre = (common * tanh_val * sigmoid_val * (1.0 - sigmoid_val)).astype(jnp.bfloat16)
    return (tanh_pre, sigmoid_pre)


def per_device(
    patch_class_features,
    live_tiles,
    tile_patient,
    ln_gain,
    up_weight,
    down_weight,
    tanh_weight,
    sigmoid_weight,
    score_weight,
    queue_keys,
    queue_labels,
    patient_labels,
    loss_scale,
):
    per_dev = patch_class_features.shape[0]
    pat_dev = patient_labels.shape[0]
    gate_dim = score_weight.shape[0]
    slot_index = lax.broadcasted_iota(jnp.int32, (per_dev,), 0)
    local_patient = jnp.where(slot_index < live_tiles[0], tile_patient, pat_dev)
    gathered, marker = (
        lax.all_gather(patch_class_features, "tile", axis=0, tiled=True),
        lax.all_gather(local_patient.astype(jnp.bfloat16), "tile", axis=0, tiled=True),
    )
    patient_all = marker.astype(jnp.int32)
    normed = layer_norm(gathered, ln_gain)
    pre_act = jnp.dot(normed, up_weight, preferred_element_type=jnp.float32)
    hidden_act = gelu_value(pre_act).astype(jnp.bfloat16)
    mlp_terms = jnp.dot(hidden_act, down_weight, preferred_element_type=jnp.float32)
    mixed_rows = lax.psum_scatter(
        mlp_terms.astype(jnp.bfloat16), "tile", scatter_dimension=0, tiled=True
    ).astype(jnp.float32)
    start_row = lax.axis_index("tile") * per_dev
    tile_state = (
        lax.dynamic_slice_in_dim(gathered, start_row, per_dev, 0).astype(jnp.float32) + mixed_rows
    )
    row_patient = lax.dynamic_slice_in_dim(patient_all, start_row, per_dev, 0)
    tanh_full, sigmoid_full = (
        lax.all_gather(tanh_weight, "tile", axis=0, tiled=True),
        lax.all_gather(sigmoid_weight, "tile", axis=0, tiled=True),
    )
    head_in = tile_state.astype(jnp.bfloat16)
    both_pre = jnp.dot(
        head_in,
        jnp.concatenate([tanh_full, sigmoid_full], axis=1),
        preferred_element_type=jnp.float32,
    )
    tanh_val = jnp.tanh(both_pre[:, :gate_dim])
    sigmoid_val = jax.nn.sigmoid(both_pre[:, gate_dim:])
    gate_product = tanh_val * sigmoid_val
    tile_score = jnp.sum(gate_product * score_weight, axis=1)
    onehot = (row_patient[:, None] == lax.broadcasted_iota(jnp.int32, (1, pat_dev), 1)).astype(
        jnp.float32
    )
    pool_mass = onehot * jnp.exp(tile_score)[:, None]
    vectors = jnp.einsum("rp,rd->pd", pool_mass, tile_state, precision=highest)
    total_mass, vectors = lax.psum((jnp.sum(pool_mass, axis=0), vectors), "tile")
    pooled = vectors / total_mass[:, None]
    length = jnp.sqrt(jnp.sum(pooled * pooled, axis=1) + 1e-06)
    rescaled_bag_embedding = pooled / length[:, None]
    key_squares = jnp.einsum("kd,kd->k", queue_keys, queue_keys, preferred_element_type=jnp.float32)
    direction_queue_entry = (queue_keys * lax.rsqrt(key_squares + 1e-06)[:, None]).astype(
        jnp.bfloat16
    )
    cosine_match_scores = (
        jnp.einsum(
            "pd,kd->pk",
            rescaled_bag_embedding.astype(jnp.bfloat16),
            direction_queue_entry,
            preferred_element_type=jnp.float32,
        )
        / sharpness_divisor
    )
    same_label = (patient_labels[:, None] == queue_labels[None, :]).astype(jnp.float32)
    exp_logits = jnp.exp(cosine_match_scores)
    exp_total, positive_sum, positives = lax.psum(
        (
            jnp.sum(exp_logits, axis=1),
            jnp.sum(same_label * cosine_match_scores, axis=1),
            jnp.sum(same_label, axis=1),
        ),
        "tile",
    )
    loss_part = jnp.sum(jnp.log(exp_total) - positive_sum / positives)
    score_derivative_lines = (
        loss_scale * (exp_logits / exp_total[:, None] - same_label / positives[:, None])
    ).astype(jnp.bfloat16)
    rescaled_derivative = (
        lax.psum(
            jnp.dot(
                score_derivative_lines, direction_queue_entry, preferred_element_type=jnp.float32
            ),
            "tile",
        )
        / sharpness_divisor
    )
    pooled_grad = (
        rescaled_derivative
        - rescaled_bag_embedding
        * jnp.sum(rescaled_bag_embedding * rescaled_derivative, axis=1, keepdims=True)
    ) / length[:, None]
    alpha_row = jnp.sum(pool_mass / total_mass[None, :], axis=1)
    row_grad = jnp.dot(onehot, pooled_grad, precision=highest)
    row_center = jnp.dot(onehot, pooled, precision=highest)
    score_grads = alpha_row * jnp.sum((tile_state - row_center) * row_grad, axis=1)
    tanh_pre, sigmoid_pre = gate_backward(score_grads, tanh_val, sigmoid_val, score_weight)
    state_grad = (
        alpha_row[:, None] * row_grad
        + jnp.einsum("rl,dl->rd", tanh_pre, tanh_full, preferred_element_type=jnp.float32)
        + jnp.einsum("rl,dl->rd", sigmoid_pre, sigmoid_full, preferred_element_type=jnp.float32)
    )
    out_grads = lax.all_gather(state_grad.astype(jnp.bfloat16), "tile", axis=0, tiled=True)
    tanh_part, sigmoid_part = (
        lax.psum_scatter(
            jnp.einsum("rd,rl->dl", head_in, tanh_pre, preferred_element_type=jnp.float32).astype(
                jnp.bfloat16
            ),
            "tile",
            scatter_dimension=0,
            tiled=True,
        ).astype(jnp.float32),
        lax.psum_scatter(
            jnp.einsum(
                "rd,rl->dl", head_in, sigmoid_pre, preferred_element_type=jnp.float32
            ).astype(jnp.bfloat16),
            "tile",
            scatter_dimension=0,
            tiled=True,
        ).astype(jnp.float32),
    )
    score_part = lax.psum(jnp.sum(score_grads[:, None] * gate_product, axis=0), "tile")
    hidden_grad = jnp.einsum(
        "rd,fd->rf", out_grads, down_weight, preferred_element_type=jnp.float32
    )
    pre_grad = (hidden_grad * gelu_slope(pre_act)).astype(jnp.bfloat16)
    up_part = jnp.einsum("rd,rf->df", normed, pre_grad, preferred_element_type=jnp.float32)
    down_part = jnp.einsum("rf,rd->fd", hidden_act, out_grads, preferred_element_type=jnp.float32)
    up_grad, down_grad = (
        lax.psum_scatter(
            up_part.astype(jnp.bfloat16), "pat", scatter_dimension=0, tiled=True
        ).astype(jnp.float32),
        lax.psum_scatter(
            down_part.astype(jnp.bfloat16), "pat", scatter_dimension=1, tiled=True
        ).astype(jnp.float32),
    )
    tanh_grad, sigmoid_grad, score_grad, contrastive_loss = (
        lax.psum(tanh_part.astype(jnp.bfloat16), "pat").astype(jnp.float32),
        lax.psum(sigmoid_part.astype(jnp.bfloat16), "pat").astype(jnp.float32),
        lax.psum(score_part.astype(jnp.bfloat16), "pat").astype(jnp.float32),
        lax.psum(loss_part.astype(jnp.bfloat16), "pat").astype(jnp.float32),
    )
    return (up_grad, down_grad, tanh_grad, sigmoid_grad, score_grad, contrastive_loss)


def solution(mesh):
    placed = (
        P(("pat", "tile"), None),
        P(("pat", "tile")),
        P(("pat", "tile")),
        P(),
        P(None, "tile"),
        P("tile", None),
        P("tile", None),
        P("tile", None),
        P(),
        P("tile", None),
        P("tile"),
        P("pat"),
        P(),
    )
    return jax.shard_map(
        per_device,
        mesh=mesh,
        in_specs=placed,
        out_specs=(P("pat", "tile"), P("tile", "pat"), P("tile", None), P("tile", None), P(), P()),
        check_vma=False,
    )
```

profile of v0, /device:TPU:32, one launch (start us, length us, event | category | flops | bytes accessed | tf_op | source)
XLA Modules:
  0.0 1245.3 jit_solution(326035553945307576)
XLA Ops:
  8.0 120.7 %all-gather.4.cloned.1.call-done = bf16[2048,1536]{1,0:T(8,128)(2,1)} async-done(((bf16[128,1536]{1,0:T(8,128)(2,1)}), bf16[2048,1536]{1,0:T(8,128)(2,1)}) %all-gather.4.cloned.1.call-update) | async-done | bytes 6291472 | tf_op jit(solution)/shard_map/all_gather | solution.py:56
  128.7 3.8 convert_reduce_fusion
  135.1 2.3 fusion.4
  137.5 5.4 multiply_convert_fusion
  144.1 5.3 convolution_convert_fusion
  150.1 35.4 %all-gather = bf16[16,1,128]{2,1,0:T(2,128)(2,1)S(1)} all-gather(bf16[1,1,128]{2,1,0:T(2,128)(2,1)S(1)} %fusion.66), channel_id=1, replica_groups=mesh['pat'=16,'tile'=16] {'tile'}, dimensions={0}, use_global_device_ids=true | all-gather | bytes 4352 | tf_op jit(solution)/shard_map/all_gather | solution.py:57
  185.6 2.6 fusion.6
  188.8 44.6 %all_gather.18 = bf16[1536,256]{1,0:T(8,128)(2,1)S(1)} all-gather(bf16[96,256]{1,0:T(8,128)(2,1)S(1)} %copy-done.5), channel_id=1, replica_groups=mesh['pat'=16,'tile'=16] {'tile'}, dimensions={0}, use_global_device_ids=true | all-gather | bytes 835584 | tf_op jit(solution)/shard_map/all_gather | solution.py:74
  233.4 43.1 %all_gather.17 = bf16[1536,256]{1,0:T(8,128)(2,1)S(1)} all-gather(bf16[96,256]{1,0:T(8,128)(2,1)S(1)} %copy-done.6), channel_id=1, replica_groups=mesh['pat'=16,'tile'=16] {'tile'}, dimensions={0}, use_global_device_ids=true | all-gather | bytes 835584 | tf_op jit(solution)/shard_map/all_gather | solution.py:73
  276.5 94.5 %reduce-scatter.6.cloned.1.call-done = bf16[128,1536]{1,0:T(8,128)(2,1)} async-done(((bf16[2048,1536]{1,0:T(8,128)(2,1)}), bf16[128,1536]{1,0:T(8,128)(2,1)}) %reduce-scatter.6.cloned.1.call-update) | async-done | bytes 393232 | tf_op jit(solution)/shard_map/reduce_scatter | solution.py:64
  376.9 72.3 %all-reduce.2 = (f32[4]{0:T(128)S(1)}, f32[4,1536]{1,0:T(4,128)}) all-reduce(f32[4]{0:T(128)} %select_reduce_fusion, f32[4,1536]{1,0:T(4,128)} %fusion.27), channel_id=1, replica_groups=mesh['pat'=16,'tile'=16] {'tile'}, use_global_device_ids=true, to_apply=%region_5.6 | all-reduce | flops 6148 | bytes 49184 | tf_op jit(solution)/shard_map/psum | solution.py:91
  451.2 4.2 fusion.46
  455.5 37.4 %all-reduce.1 = (f32[4]{0:T(128)}, f32[4]{0:T(128)}) all-reduce(f32[4]{0:T(128)} %get-tuple-element.8, f32[4]{0:T(128)} %get-tuple-element.7), channel_id=1, replica_groups=mesh['pat'=16,'tile'=16] {'tile'}, use_global_device_ids=true, to_apply=%region_12.13 | all-reduce | flops 8 | bytes 64 | tf_op jit(solution)/shard_map/psum | solution.py:110
  492.9 3.2 fusion.19
  496.1 75.3 %psum.81 = f32[4,1536]{1,0:T(4,128)} all-reduce(f32[4,1536]{1,0:T(4,128)} %fusion.19), channel_id=1, replica_groups=mesh['pat'=16,'tile'=16] {'tile'}, use_global_device_ids=true, to_apply=%region_13.14 | all-reduce | flops 6144 | bytes 49152 | tf_op jit(solution)/shard_map/psum | solution.py:123
  582.2 114.9 %all-gather.6.cloned.1.call-done = bf16[2048,1536]{1,0:T(8,128)(2,1)} async-done(((bf16[128,1536]{1,0:T(8,128)(2,1)}), bf16[2048,1536]{1,0:T(8,128)(2,1)}) %all-gather.6.cloned.1.call-update) | async-done | bytes 6291472 | tf_op jit(solution)/shard_map/all_gather | solution.py:146
  697.0 13.6 %convolution_convert_fusion.2 = bf16[1536,384]{1,0:T(8,128)(2,1)} fusion(bf16[2048,1536]{1,0:T(8,128)(2,1)} %copy-done.2, f32[2048,384]{1,0:T(8,128)} %get-tuple-element.25, bf16[2048,1536]{1,0:T(8,128)(2,1)} %all-gather.6.cloned.1.call-done, bf16[384,1536]{1,0:T(8,128)(2,1)S(1)} %copy-done), kind=kOutput, calls=%fused_computation.22 | convolution fusion | flops 4840292352 | bytes 18087936 | tf_op jit(solution)/shard_map/rd,rf->df/dot_general | solution.py:170
  710.9 7.3 convolution_convert_fusion.1
  718.2 36.8 %all-reduce = (bf16[256]{0:T(256)(128)(2,1)S(1)}, f32[4]{0:T(128)S(1)}) all-reduce(f32[256]{0:T(256)S(1)} %get-tuple-element.21, f32[4]{0:T(128)S(1)} %copy-done.13), channel_id=1, replica_groups=mesh['pat'=16,'tile'=16] {'tile'}, use_global_device_ids=true, to_apply=%region_23.24 | all-reduce | flops 260 | bytes 1568 | tf_op jit(solution)/shard_map/psum | solution.py:165
  755.6 144.5 %reduce-scatter.12.cloned.1.call-done = bf16[96,256]{1,0:T(8,128)(2,1)} async-done(((bf16[1536,256]{1,0:T(8,128)(2,1)}), bf16[96,256]{1,0:T(8,128)(2,1)}) %reduce-scatter.12.cloned.1.call-update) | async-done | bytes 49168 | tf_op jit(solution)/shard_map/reduce_scatter | solution.py:148
  900.1 204.3 %reduce-scatter.14.cloned.1.call-done = bf16[96,256]{1,0:T(8,128)(2,1)} async-done(((bf16[1536,256]{1,0:T(8,128)(2,1)}), bf16[96,256]{1,0:T(8,128)(2,1)}) %reduce-scatter.14.cloned.1.call-update) | async-done | bytes 49168 | tf_op jit(solution)/shard_map/reduce_scatter | solution.py:156
  1104.4 54.2 %all-reduce.5 = (bf16[96,256]{1,0:T(8,128)(2,1)S(1)}, bf16[96,256]{1,0:T(8,128)(2,1)S(1)}, bf16[256]{0:T(256)(128)(2,1)S(1)}, bf16[]{:T(256)}) all-reduce(bf16[96,256]{1,0:T(8,128)(2,1)} %reduce-scatter.12.cloned.1.call-done, bf16[96,256]{1,0:T(8,128)(2,1)} %reduce-scatter.14.cloned.1.call-done, ...), channel_id=1, replica_groups=mesh['pat'=16,'tile'=16] {'pat'}, use_global_device_ids=true, to_apply=%region_19.20 | all-reduce | flops 49409 | bytes 197636 | tf_op jit(solution)/shard_map/psum | solution.py:181
  1161.2 9.0 reduce-scatter.8.cloned.1.call-done
  1171.7 64.1 %reduce-scatter.10.cloned.1.call-done = bf16[384,96]{0,1:T(8,128)(2,1)} async-done(((bf16[384,1536]{0,1:T(8,128)(2,1)}), bf16[384,96]{0,1:T(8,128)(2,1)}) %reduce-scatter.10.cloned.1.call-update) | async-done | bytes 73744 | tf_op jit(solution)/shard_map/reduce_scatter | solution.py:176
  (77 shorter events, 29.3 us)
Async XLA Ops:
  7.2 136.9 %copy-start = (bf16[384,1536]{1,0:T(8,128)(2,1)S(1)}, bf16[384,1536]{1,0:T(8,128)(2,1)}, u32[]{:S(2)}) copy-start(bf16[384,1536]{1,0:T(8,128)(2,1)} %param.18) | copy-start | bytes 3538948
  7.2 121.5 %all-gather.4.cloned.1.call-start = ((), (), s32[]{:S(2)}) async-start(), calls=%async_computation.5 | async-start | bytes 6684672 | tf_op jit(solution)/shard_map/all_gather | solution.py:56
  7.9 363.0 %reduce-scatter.6.cloned.1.call-start = ((), (), s32[]{:S(2)}) async-start(), calls=%async_computation.6 | async-start | bytes 6684672 | tf_op jit(solution)/shard_map/reduce_scatter | solution.py:64
  128.7 4.6 copy-start.1
  133.3 1.8 copy-start.7
  135.1 2.4 copy-start.11
  137.5 5.4 copy-start.2
  142.9 1.2 copy-start.14
  149.3 0.8 copy-start.12
  149.4 39.4 %copy-start.5 = (bf16[96,256]{1,0:T(8,128)(2,1)S(1)}, bf16[96,256]{1,0:T(8,128)(2,1)}, u32[]{:S(2)}) copy-start(bf16[96,256]{1,0:T(8,128)(2,1)} %param.20) | copy-start | bytes 147460
  149.4 84.0 %copy-start.6 = (bf16[96,256]{1,0:T(8,128)(2,1)S(1)}, bf16[96,256]{1,0:T(8,128)(2,1)}, u32[]{:S(2)}) copy-start(bf16[96,256]{1,0:T(8,128)(2,1)} %param.19) | copy-start | bytes 147460
  149.4 547.6 %all-gather.6.cloned.1.call-start = ((), (), s32[]{:S(2)}) async-start(), calls=%async_computation.7 | async-start | bytes 6684672 | tf_op jit(solution)/shard_map/all_gather | solution.py:146
  188.2 185.1 %copy-start.8 = (f32[256]{0:T(256)S(1)}, f32[256]{0:T(256)}, u32[]{:S(2)}) copy-start(f32[256]{0:T(256)} %param.21) | copy-start | bytes 3076
  370.9 3.1 copy-start.3
  372.6 0.7 copy-start.4
  579.4 320.7 %reduce-scatter.12.cloned.1.call-start = ((), (), s32[]{:S(2)}) async-start(), calls=%async_computation.10 | async-start | bytes 835584 | tf_op jit(solution)/shard_map/reduce_scatter | solution.py:148
  580.7 523.7 %reduce-scatter.14.cloned.1.call-start = ((), (), s32[]{:S(2)}) async-start(), calls=%async_computation.11 | async-start | bytes 835584 | tf_op jit(solution)/shard_map/reduce_scatter | solution.py:156
  582.1 588.0 %reduce-scatter.8.cloned.1.call-start = ((), (), s32[]{:S(2)}) async-start(), calls=%async_computation.8 | async-start | bytes 1253376 | tf_op jit(solution)/shard_map/reduce_scatter | solution.py:173
  697.0 13.9 %copy-start.15 = (bf16[2048,384]{1,0:T(8,128)(2,1)S(1)}, bf16[2048,384]{1,0:T(8,128)(2,1)}, u32[]{:S(2)}) copy-start(bf16[2048,384]{1,0:T(8,128)(2,1)} %copy-done.14) | copy-start | bytes 4718596
  710.6 7.6 copy-start.13
  710.6 44.4 %copy-start.9 = (f32[4]{0:T(128)S(1)}, f32[4]{0:T(128)}, u32[]{:S(2)}) copy-start(f32[4]{0:T(128)} %get-tuple-element.11) | copy-start | bytes 52
  710.6 44.4 %copy-start.10 = (f32[4]{0:T(128)S(1)}, f32[4]{0:T(128)}, u32[]{:S(2)}) copy-start(f32[4]{0:T(128)} %get-tuple-element.12) | copy-start | bytes 52
  710.6 525.1 %reduce-scatter.10.cloned.1.call-start = ((), (), s32[]{:S(2)}) async-start(), calls=%async_computation.9 | async-start | bytes 1253376 | tf_op jit(solution)/shard_map/reduce_scatter | solution.py:176
Sparse Core Ops, SparseCore 0:
  10.6 118.0 all-gather.3
  149.5 221.4 reduce-scatter.5
  579.5 117.4 all-gather.5
  701.2 198.8 reduce-scatter.11
  903.8 200.5 reduce-scatter.13
  1107.0 63.1 reduce-scatter.7
  1172.8 62.9 reduce-scatter.9
where the time goes:
time: 1250 us
  waiting for transfers between devices  753 us (60%)
  blocking collectives  399 us (32%)
  matrix products  49.3 us (4%)
  other arithmetic  23.6 us (2%)
  between operations  17.4 us (1%)
    reduce_scatter x1, waiting for transfers between devices, per_device(): lax.psum_scatter(jnp.einsum('rd,rl->dl', head_in, sigmoid_pre, preferred_...  204 us
    reduce_scatter x1, waiting for transfers between devices, per_device(): lax.psum_scatter(jnp.einsum('rd,rl->dl', head_in, tanh_pre, preferred_ele...  145 us
    all_gather x1, waiting for transfers between devices, per_device(): lax.all_gather(patch_class_features, 'tile', axis=0, tiled=True)  121 us
    all_gather x1, waiting for transfers between devices, per_device(): lax.all_gather(state_grad.astype(jnp.bfloat16), 'tile', axis=0, tiled=True)  115 us
    reduce_scatter x1, waiting for transfers between devices, per_device(): lax.psum_scatter(mlp_terms.astype(jnp.bfloat16), 'tile', scatter_dimensio...  94.5 us
    psum x1, blocking collectives, per_device(): lax.psum(jnp.dot(score_derivative_lines, direction_queue_entry, preferred...  75.3 us
    psum x1, blocking collectives, per_device(): lax.psum((jnp.sum(pool_mass, axis=0), vectors), 'tile')  72.3 us
    reduce_scatter x1, waiting for transfers between devices, per_device(): lax.psum_scatter(down_part.astype(jnp.bfloat16), 'pat', scatter_dimension...  64.1 us
  transfers between devices with their start and end apart: 7, of which 7 were waited for; matrix products, arithmetic and copies ran while one was open for 2% of the time, Pallas kernels for 0%

commit v1 on v0

v1 whole, which is shorter than its diff:
```python
import jax
import jax.numpy as jnp
from jax import lax
from jax.experimental import pallas as pl
from jax.experimental.pallas import tpu as pltpu
from jax.sharding import PartitionSpec as P

MESH = pl.DeviceIdType.MESH
F32 = jnp.float32
BF16 = jnp.bfloat16
HIGH = lax.Precision.HIGHEST
INV_TEMP = 1.0 / 0.07
NZ = 8
NY = 4
NX = 4
ROWS = 128
TOK = NZ * ROWS
D = 1536
HID = 384
GATE = 256
VMEM_LIMIT = 56 << 20


class Place:
    def __init__(self):
        self.pat = lax.axis_index("pat")
        self.tile = lax.axis_index("tile")
        self.z = lax.div(self.tile, 2)
        self.q = lax.rem(self.tile, 2)
        self.xl = lax.div(self.pat, 8)
        self.y = lax.rem(lax.div(self.pat, 2), 4)
        self.c = lax.rem(self.pat, 2)
        self.x = self.q * 2 + self.xl

    def at(self, z=None, y=None, x=None, c=None):
        z = self.z if z is None else z
        y = self.y if y is None else y
        c = self.c if c is None else c
        if x is None:
            xl, q = self.xl, self.q
        else:
            xl, q = lax.rem(x, 2), lax.div(x, 2)
        return (xl * 8 + y * 2 + c, z * 2 + q)

    def dz(self, d):
        return lax.rem(self.z + (d + NZ), NZ)

    def dy(self, d):
        return lax.rem(self.y + (d + NY), NY)

    def dx(self, d):
        return lax.rem(self.x + (d + NX), NX)


def meet(partners):
    barrier = pltpu.get_barrier_semaphore()
    for device in partners:
        pl.semaphore_signal(barrier, inc=1, device_id=device, device_id_type=MESH)
    pl.semaphore_wait(barrier, len(partners))


class Mail:
    def __init__(self, send_sem, recv_sem):
        self.send_sem, self.recv_sem = send_sem, recv_sem
        self.next = 0
        self.sent = []

    def slots(self, n):
        first = self.next
        self.next += n
        return first

    def send(self, k, src, dst, device):
        copy = pltpu.make_async_remote_copy(
            src_ref=src, dst_ref=dst, send_sem=self.send_sem.at[k], recv_sem=self.recv_sem.at[k],
            device_id=device, device_id_type=MESH,
        )
        copy.start()
        self.sent.append(copy)

    def arrive(self, k, dst, device):
        pltpu.make_async_remote_copy(
            src_ref=dst, dst_ref=dst, send_sem=self.send_sem.at[k], recv_sem=self.recv_sem.at[k],
            device_id=device, device_id_type=MESH,
        ).wait_recv()

    def finish(self):
        for copy in self.sent:
            copy.wait_send()


def rows_at(index, size, offset=0, count=None):
    count = size if count is None else count
    return pl.ds(pl.multiple_of(index * size + offset, 16), count)


def lanes_at(index, size):
    return pl.ds(pl.multiple_of(index * size, 128), size)


class ZGather:
    def __init__(self, mail, place, ref, own, size):
        self.mail, self.place, self.ref, self.own, self.size = mail, place, ref, own, size
        self.half = size // 2
        self.key = mail.slots(16)
        self.chains = ((1, 0, 4), (-1, 1, 4), (1, 1, 3), (-1, 0, 3))

    def piece(self, owner, half):
        return self.ref.at[rows_at(owner, self.size, half * self.half, self.half)]

    def step(self, s):
        p = self.place
        for i, (way, half, steps) in enumerate(self.chains):
            if s > 0 and s <= steps:
                self.mail.arrive(self.key + i * 4 + s - 1, self.piece(p.dz(-way * s), half), p.at(z=p.dz(-way)))
            if s < steps:
                dst = self.piece(p.dz(-way * s), half)
                if s == 0:
                    src = self.own.at[pl.ds(half * self.half, self.half)]
                else:
                    src = dst
                self.mail.send(self.key + i * 4 + s, src, dst, p.at(z=p.dz(way)))


class ZReduce:
    def __init__(self, mail, place, ref, size, stage, recv):
        self.mail, self.place, self.ref, self.size = mail, place, ref, size
        self.stage, self.recv = stage, recv
        self.half = size // 2
        self.key = mail.slots(16)
        self.chains = ((1, 0, 4), (-1, 1, 4), (1, 1, 3), (-1, 0, 3))

    def piece(self, owner, half):
        return rows_at(owner, self.size, half * self.half, self.half)

    def step(self, s):
        p = self.place
        for i, (way, half, steps) in enumerate(self.chains):
            if s < steps:
                dest = self.piece(p.dz(way * (steps - s)), half)
                if s == 0:
                    src = self.ref.at[dest]
                else:
                    self.mail.arrive(self.key + i * 4 + s - 1, self.recv.at[i, s - 1], p.at(z=p.dz(-way)))
                    src = self.stage.at[i, s - 1]
                    src[...] = (self.ref[dest].astype(F32) + self.recv[i, s - 1].astype(F32)).astype(BF16)
                self.mail.send(self.key + i * 4 + s, src, self.recv.at[i, s], p.at(z=p.dz(way)))

    def total(self):
        p = self.place
        for i, (way, half, steps) in enumerate(self.chains):
            self.mail.arrive(self.key + i * 4 + steps - 1, self.recv.at[i, steps - 1], p.at(z=p.dz(-way)))
        first = self.ref[self.piece(p.z, 0)].astype(F32) + self.recv[0, 3].astype(F32) + self.recv[3, 2].astype(F32)
        second = self.ref[self.piece(p.z, 1)].astype(F32) + self.recv[1, 3].astype(F32) + self.recv[2, 2].astype(F32)
        return jnp.concatenate([first, second], axis=0)


class Swap:
    def __init__(self, mail, ref, me, n, device_of):
        self.mail, self.ref, self.me, self.n, self.device_of = mail, ref, me, n, device_of
        self.key = mail.slots(n - 1)

    def other(self, d):
        return lax.rem(self.me + d, self.n)

    def start(self):
        for d in range(1, self.n):
            mine = self.ref.at[self.me]
            self.mail.send(self.key + d - 1, mine, mine, self.device_of(self.other(d)))

    def wait(self):
        for d in range(1, self.n):
            source = self.other(self.n - d)
            self.mail.arrive(self.key + d - 1, self.ref.at[source], self.device_of(source))

    def total(self):
        self.wait()
        value = self.ref[0].astype(F32)
        for j in range(1, self.n):
            value = value + self.ref[j].astype(F32)
        return value


def gather_kernel(nm, up, dn, wg, n_all, up_all, dn_all, w_all, send_sem, recv_sem, local_sem):
    p = Place()
    mail = Mail(send_sem, recv_sem)
    beside = p.at(x=3 - p.x)
    mate = p.at(c=1 - p.c)
    above, below = p.at(y=p.dy(1)), p.at(y=p.dy(-1))
    meet([p.at(z=p.dz(1)), p.at(z=p.dz(-1)), beside, mate, above, below])
    tokens = ZGather(mail, p, n_all, nm, ROWS)
    tokens.step(0)

    def w_block(z, q, y):
        return w_all.at[pl.ds(pl.multiple_of(z * 192 + q * 96, 96), 96), lanes_at(y, 128)]

    def up_half(q, c):
        return up_all.at[rows_at(c, 768), lanes_at(q, HID)]

    def dn_half(q, c):
        return dn_all.at[pl.ds(pl.multiple_of(q * HID + c * 192, 192), 192)]

    k_w = mail.slots(1)
    mail.send(k_w, wg.at[:, lanes_at(p.y, 128)], w_block(p.z, p.q, p.y), beside)
    k_half = mail.slots(2)
    mail.send(k_half, up.at[rows_at(p.c, 768)], up_half(p.q, p.c), beside)
    mail.send(k_half + 1, dn.at[rows_at(p.c, 192)], dn_half(p.q, p.c), beside)
    locals_ = [
        pltpu.make_async_copy(wg.at[:, lanes_at(p.y, 128)], w_block(p.z, p.q, p.y), local_sem.at[0]),
        pltpu.make_async_copy(nm, n_all.at[rows_at(p.z, ROWS)], local_sem.at[1]),
        pltpu.make_async_copy(up, up_all.at[:, lanes_at(p.q, HID)], local_sem.at[2]),
        pltpu.make_async_copy(dn, dn_all.at[rows_at(p.q, HID)], local_sem.at[3]),
    ]
    for copy in locals_:
        copy.start()
    locals_[0].wait()
    mail.arrive(k_w, w_block(p.z, 1 - p.q, p.y), beside)
    k_z = mail.slots(7)

    def w_rows(z):
        return w_all.at[pl.ds(pl.multiple_of(z * 192, 192), 192), lanes_at(p.y, 128)]

    def gate_step(s):
        for way, steps, key in ((1, 4, k_z), (-1, 3, k_z + 4)):
            if s > 0 and s <= steps:
                mail.arrive(key + s - 1, w_rows(p.dz(-way * s)), p.at(z=p.dz(-way)))
            if s < steps:
                block = w_rows(p.dz(-way * s))
                mail.send(key + s, block, block, p.at(z=p.dz(way)))

    gate_step(0)
    for s in range(1, 4):
        tokens.step(s)
        gate_step(s)
    gate_step(4)

    def w_lanes(y, half=None):
        if half is None:
            return w_all.at[:, lanes_at(y, 128)]
        return w_all.at[pl.ds(half * 768, 768), lanes_at(y, 128)]

    k_y = mail.slots(4)
    mail.send(k_y, w_lanes(p.y), w_lanes(p.y), above)
    mail.send(k_y + 1, w_lanes(p.y), w_lanes(p.y), below)
    k_mate = mail.slots(2)
    theirs, other = 1 - p.q, 1 - p.c
    mail.arrive(k_half, up_half(theirs, p.c), beside)
    mail.send(k_mate, up_half(theirs, p.c), up_half(theirs, p.c), mate)
    mail.arrive(k_half + 1, dn_half(theirs, p.c), beside)
    mail.send(k_mate + 1, dn_half(theirs, p.c), dn_half(theirs, p.c), mate)
    mail.arrive(k_y, w_lanes(p.dy(-1)), below)
    mail.send(k_y + 2, w_lanes(p.dy(-1), 0), w_lanes(p.dy(-1), 0), above)
    mail.arrive(k_y + 1, w_lanes(p.dy(1)), above)
    mail.send(k_y + 3, w_lanes(p.dy(1), 1), w_lanes(p.dy(1), 1), below)
    tokens.step(4)
    mail.arrive(k_y + 2, w_lanes(p.dy(2), 0), below)
    mail.arrive(k_y + 3, w_lanes(p.dy(2), 1), above)
    mail.arrive(k_mate, up_half(theirs, other), mate)
    mail.arrive(k_mate + 1, dn_half(theirs, other), mate)
    for copy in locals_[1:]:
        copy.wait()
    mail.finish()


ANY = pl.BlockSpec(memory_space=pl.ANY)
VMEM = pl.BlockSpec(memory_space=pltpu.VMEM)


def shape(dims, dtype):
    return jax.ShapeDtypeStruct(dims, dtype)


def gather(nm, up, dn, wg):
    return pl.pallas_call(
        gather_kernel,
        name="gather",
        out_shape=(
            shape((TOK, D), BF16),
            shape((D, 2 * HID), BF16),
            shape((2 * HID, D), BF16),
            shape((D, 2 * GATE), BF16),
        ),
        in_specs=[ANY] * 4,
        out_specs=(ANY,) * 4,
        scratch_shapes=[
            pltpu.SemaphoreType.DMA((32,)),
            pltpu.SemaphoreType.DMA((32,)),
            pltpu.SemaphoreType.DMA((4,)),
        ],
        compiler_params=pltpu.CompilerParams(collective_id=1, has_side_effects=True),
    )(nm, up, dn, wg)


def two_part(a):
    top = a.astype(BF16).astype(F32)
    return jnp.concatenate([top, a - top], axis=0).astype(BF16)


def dot_two(a, b, transposed=False):
    dims = (((1,), (1,)), ((), ())) if transposed else (((1,), (0,)), ((), ()))
    both = lax.dot_general(two_part(a), b, dims, preferred_element_type=F32)
    half = a.shape[0]
    return both[:half] + both[half:]


def head_kernel(
    part, x_ref, w_ref, h_ref, dn_ref, key_ref, qlab_ref, plab_ref, marker_ref, sw_ref, scale_ref,
    uv_all, score_all, alpha_all, pm_all, grad_out, misc,
    uv_own, stage, recv, pbuf, zbuf, xbuf, sbuf, send_sem, recv_sem,
):
    p = Place()
    mail = Mail(send_sem, recv_sem)
    z_dev = lambda z: p.at(z=z)
    q_dev = lambda q: (p.pat, p.z * 2 + q)
    meet([p.at(z=p.dz(d)) for d in range(1, NZ)] + [q_dev(1 - p.q)])
    reduce = ZReduce(mail, p, part, ROWS, stage, recv)
    gather_uv = ZGather(mail, p, uv_all, uv_own, ROWS)
    swap_p = Swap(mail, pbuf, p.z, NZ, z_dev)
    swap_z = [Swap(mail, zbuf.at[i], p.z, NZ, z_dev) for i in range(3)]
    swap_x = [Swap(mail, xbuf.at[i], p.q, 2, q_dev) for i in range(3)]
    swap_s = Swap(mail, sbuf, p.z, NZ, z_dev)

    row8 = lax.broadcasted_iota(jnp.int32, (8, 128), 0)
    first4 = row8 < 4
    first4_wide = lax.broadcasted_iota(jnp.int32, (8, 768), 0) < 4
    lane = lax.broadcasted_iota(jnp.int32, (8, 128), 1)

    def pack(v):
        return jnp.where(first4_wide, v[:, :768], v[:, 768:])

    def unpack(v):
        other = pltpu.roll(v, 4, 0)
        return jnp.concatenate([jnp.where(first4_wide, v, other), jnp.where(first4_wide, other, v)], axis=1)

    reduce.step(0)
    gate_x = jnp.dot(x_ref[...], w_ref[...], preferred_element_type=F32)
    reduce.step(1)
    same = (plab_ref[...] == qlab_ref[...]).astype(F32)
    label_sums = jnp.dot(same.astype(BF16), key_ref[...], preferred_element_type=F32)
    positives = jnp.sum(same, axis=1, keepdims=True)
    reduce.step(2)
    reduce.step(3)
    gates = reduce.total() + gate_x
    tanh_val = jnp.tanh(gates[:, :GATE])
    sigmoid_val = jax.nn.sigmoid(gates[:, GATE:])
    product = tanh_val * sigmoid_val
    sw = sw_ref[...]
    score = lax.dot_general(
        jnp.broadcast_to(sw, (8, GATE)), product, (((1,), (1,)), ((), ())), precision=HIGH, preferred_element_type=F32
    )
    onehot = marker_ref[...] == lax.rem(row8, 4)
    mass = jnp.where(onehot, jnp.exp(score), 0.0)
    pbuf[p.z] = mass
    swap_p.start()
    common = sw * sigmoid_val
    uv_own[:, :GATE] = (common * (1.0 - tanh_val * tanh_val)).astype(BF16)
    uv_own[:, GATE:] = (common * tanh_val * (1.0 - sigmoid_val)).astype(BF16)
    gather_uv.step(0)
    uv_all[rows_at(p.z, ROWS)] = uv_own[...]
    vec_x = dot_two(mass, x_ref[...])
    swap_p.wait()

    held = jnp.zeros((8, 2 * HID), F32)
    total = jnp.zeros((8, 1), F32)
    for z in range(NZ):
        block = pbuf[z]
        pm_all[z] = block
        held += dot_two(block, h_ref[pl.ds(z * ROWS, ROWS)])
        total += jnp.sum(block, axis=1, keepdims=True)
    vec = dot_two(held, dn_ref[...]) + vec_x

    def post(i, packed, small):
        zbuf[i, p.z, :, :768] = packed
        zbuf[i, p.z, :, 768:] = small
        swap_z[i].start()

    def collect_z(i):
        xbuf[i, p.q] = swap_z[i].total()
        swap_x[i].start()

    post(0, pack(vec), jnp.broadcast_to(total, (8, 128)))
    gather_uv.step(1)
    post(1, pack(label_sums), jnp.broadcast_to(positives, (8, 128)))
    collect_z(0)
    gather_uv.step(2)
    collect_z(1)
    summed = swap_x[0].total()
    total_mass = summed[:, 768:769]
    pooled = unpack(summed[:, :768]) / total_mass
    length = jnp.sqrt(jnp.sum(pooled * pooled, axis=1, keepdims=True) + 1e-06)
    unit = pooled / length

    logits = lax.dot_general(
        unit.astype(BF16), key_ref[...], (((1,), (1,)), ((), ())), preferred_element_type=F32
    ) / 0.07
    exps = jnp.exp(logits)
    exp_part = jnp.sum(exps, axis=1, keepdims=True)
    pos_part = jnp.sum(same * logits, axis=1, keepdims=True)
    post(2, pack(dot_two(exps, key_ref[...])), jnp.where(lane == 0, exp_part, pos_part))
    gather_uv.step(3)
    labels_total = swap_x[1].total()
    pos_count = labels_total[:, 768:769]
    collect_z(2)
    gather_uv.step(4)
    queue_total = swap_x[2].total()
    exp_total = queue_total[:, 768:769]
    pos_logits = queue_total[:, 769:770]
    unit_grad = (scale_ref[...] * INV_TEMP) * (
        unpack(queue_total[:, :768]) / exp_total - unpack(labels_total[:, :768]) / pos_count
    )
    pooled_grad = (unit_grad - unit * jnp.sum(unit * unit_grad, axis=1, keepdims=True)) / length
    grad_out[...] = pooled_grad

    through = dot_two(pooled_grad, dn_ref[...], True)
    own_dots = dot_two(pooled_grad, x_ref[...], True)
    for z in range(NZ):
        dots = dot_two(through, h_ref[pl.ds(z * ROWS, ROWS)], True)
        dots = dots + jnp.where(p.z == z, own_dots, 0.0)
        picked = jnp.where((pbuf[z] > 0.0) & first4, dots, 0.0)
        sbuf[p.z, pl.ds(z, 1)] = jnp.sum(picked, axis=0, keepdims=True)
    swap_s.start()
    center = jnp.sum(pooled * pooled_grad, axis=1, keepdims=True)
    log_part = jnp.log(exp_total) - pos_logits / pos_count
    loss = jnp.sum(jnp.where(first4, jnp.broadcast_to(log_part, (8, 128)), 0.0), axis=0, keepdims=True)
    for z in range(NZ):
        block = jnp.where(first4, pbuf[z], 0.0)
        alpha_all[pl.ds(z, 1)] = jnp.sum(block / total_mass, axis=0, keepdims=True)
        score_all[pl.ds(z, 1)] = jnp.sum(jnp.where(block > 0.0, center, 0.0), axis=0, keepdims=True)
    score_all[...] = alpha_all[...] * (swap_s.total() - score_all[...])
    score_part = lax.dot_general(
        jnp.broadcast_to(score_all[pl.ds(p.z, 1)], (8, ROWS)), product, (((1,), (0,)), ((), ())),
        precision=HIGH, preferred_element_type=F32,
    )
    misc[...] = jnp.where(
        row8 == 0, score_part[:, :128], jnp.where(row8 == 1, score_part[:, 128:], jnp.where(row8 == 2, loss / 16.0, 0.0))
    )
    mail.finish()


def head(part, x, w, h, dn, keys, qlab, plab, marker, sw, scale):
    return pl.pallas_call(
        head_kernel,
        name="head",
        out_shape=(
            shape((TOK, 2 * GATE), BF16),
            shape((NZ, 128), F32),
            shape((NZ, 128), F32),
            shape((NZ, 8, 128), F32),
            shape((8, D), F32),
            shape((8, 128), F32),
        ),
        in_specs=[VMEM] * 11,
        out_specs=(VMEM,) * 6,
        scratch_shapes=[
            pltpu.VMEM((ROWS, 2 * GATE), BF16),
            pltpu.VMEM((4, 3, ROWS // 2, 2 * GATE), BF16),
            pltpu.VMEM((4, 4, ROWS // 2, 2 * GATE), BF16),
            pltpu.VMEM((NZ, 8, 128), F32),
            pltpu.VMEM((3, NZ, 8, 896), F32),
            pltpu.VMEM((3, 2, 8, 896), F32),
            pltpu.VMEM((NZ, 8, 128), F32),
            pltpu.SemaphoreType.DMA((72,)),
            pltpu.SemaphoreType.DMA((72,)),
        ],
        compiler_params=pltpu.CompilerParams(collective_id=2, has_side_effects=True, vmem_limit_bytes=VMEM_LIMIT),
    )(part, x, w, h, dn, keys, qlab, plab, marker, sw, scale)


def add_into(acc, others):
    value = acc[...].astype(F32)
    for other in others:
        value = value + other[...].astype(F32)
    acc[...] = value.astype(BF16)


def ring_sum(mail, key, pos, nxt, prv, get, half, hbuf, fbuf):
    at = lambda d: lax.rem(pos + d, 4)
    mail.send(key, half(get(at(2)), 0), hbuf.at[0], nxt)
    mail.send(key + 1, half(get(at(2)), 1), hbuf.at[1], prv)
    yield
    mail.arrive(key, hbuf.at[0], prv)
    add_into(half(get(at(1)), 0), [hbuf.at[0]])
    mail.send(key + 2, get(at(1)), fbuf.at[0], nxt)
    mail.arrive(key + 1, hbuf.at[1], nxt)
    add_into(half(get(at(3)), 1), [hbuf.at[1]])
    mail.send(key + 3, get(at(3)), fbuf.at[1], prv)
    yield
    mail.arrive(key + 2, fbuf.at[0], prv)
    mail.arrive(key + 3, fbuf.at[1], nxt)


def reduce_kernel(
    up, dn, gt, misc, up_out, dn_out, gate_out, misc_out,
    up0, dn0, gt0, up_acc, dn_acc, g_acc, u_yh, u_yf, u_xh, u_xf, d_xh, d_xf, d_yh, d_yf,
    g_stage, g_recv, g_y, g_x, g_c, m_z, m_y, m_x, m_c, send_sem, recv_sem,
):
    p = Place()
    mail = Mail(send_sem, recv_sem)
    mate = p.at(c=1 - p.c)
    y_dev = lambda y: p.at(y=y)
    x_dev = lambda x: p.at(x=x)
    z_dev = lambda z: p.at(z=z)
    c_dev = lambda c: p.at(c=c)
    meet(
        [mate]
        + [y_dev(p.dy(d)) for d in (1, 2, 3)]
        + [x_dev(p.dx(d)) for d in (1, 2, 3)]
        + [z_dev(p.dz(d)) for d in range(1, NZ)]
    )
    k0 = mail.slots(3)
    mail.send(k0, gt.at[:, lanes_at(1 - p.c, GATE)], gt0, mate)
    mail.send(k0 + 1, up.at[:, 1 - p.c], up0, mate)
    mail.send(k0 + 2, dn.at[:, 1 - p.c], dn0, mate)
    q_lanes = lanes_at(p.q, HID)
    k_up, k_dn = mail.slots(8), mail.slots(8)
    rows_half = lambda ref, i: ref.at[pl.ds(i * 48, 48)]

    def first_sum(src, received, acc):
        def body(i, carry):
            acc[lax.div(i, 4), lax.rem(i, 4)] = (src[i, p.c].astype(F32) + received[i].astype(F32)).astype(BF16)
            return carry

        lax.fori_loop(0, 8, body, 0)

    def up_chain():
        yield
        mail.arrive(k0 + 1, up0, mate)
        first_sum(up, up0, up_acc)
        yield from ring_sum(
            mail, k_up, p.y, y_dev(p.dy(1)), y_dev(p.dy(-1)),
            lambda d: up_acc.at[:, d], lambda ref, i: ref.at[i], u_yh, u_yf,
        )
        add_into(up_acc.at[:, p.y], [u_yf.at[0], u_yf.at[1]])
        chunk = lambda d: up_acc.at[lax.rem(d, 2), p.y, :, lanes_at(lax.div(d, 2), HID)]
        yield from ring_sum(
            mail, k_up + 4, p.x, x_dev(p.dx(1)), x_dev(p.dx(-1)), chunk, rows_half, u_xh, u_xf
        )
        up_out[...] = chunk(p.x)[...].astype(F32) + u_xf[0].astype(F32) + u_xf[1].astype(F32)

    def dn_chain():
        yield
        mail.arrive(k0 + 2, dn0, mate)
        first_sum(dn, dn0, dn_acc)
        chunk_x = lambda d: dn_acc.at[lax.rem(d, 2), :, :, lanes_at(lax.div(d, 2), HID)]
        yield from ring_sum(
            mail, k_dn, p.x, x_dev(p.dx(1)), x_dev(p.dx(-1)),
            chunk_x, lambda ref, i: ref.at[pl.ds(i * 2, 2)], d_xh, d_xf,
        )
        add_into(chunk_x(p.x), [d_xf.at[0], d_xf.at[1]])
        chunk_y = lambda d: dn_acc.at[p.xl, d, :, q_lanes]
        yield from ring_sum(
            mail, k_dn + 4, p.y, y_dev(p.dy(1)), y_dev(p.dy(-1)), chunk_y, rows_half, d_yh, d_yf
        )
        dn_out[...] = chunk_y(p.y)[...].astype(F32) + d_yf[0].astype(F32) + d_yf[1].astype(F32)

    def gate_chain():
        zred = ZReduce(mail, p, g_acc, 192, g_stage, g_recv)
        in_y = Swap(mail, g_y, p.y, 4, y_dev)
        k_x = mail.slots(3)
        in_c = Swap(mail, g_c, p.c, 2, c_dev)
        yield
        mail.arrive(k0, gt0, mate)
        g_acc[...] = (gt[:, lanes_at(p.c, GATE)].astype(F32) + gt0[...].astype(F32)).astype(BF16)
        zred.step(0)
        for s in range(1, 4):
            yield
            zred.step(s)
        yield
        g_y[p.y] = zred.total().astype(BF16)
        in_y.start()
        yield
        in_y.wait()

        def row_sum(q):
            rows = pl.ds(pl.multiple_of(q * 96, 96), 96)
            value = g_y[0, rows].astype(F32)
            for j in range(1, 4):
                value = value + g_y[j, rows].astype(F32)
            return value.astype(BF16)

        g_x[0] = row_sum(p.q)
        for d in (1, 2, 3):
            there = p.dx(d)
            g_x[4 + d] = row_sum(lax.div(there, 2))
            mail.send(k_x + d - 1, g_x.at[4 + d], g_x.at[d], x_dev(there))
        yield
        for d in (1, 2, 3):
            mail.arrive(k_x + d - 1, g_x.at[d], x_dev(p.dx(-d)))
        value = g_x[0].astype(F32)
        for d in (1, 2, 3):
            value = value + g_x[d].astype(F32)
        g_c[p.c] = value.astype(BF16)
        in_c.start()
        yield
        in_c.wait()
        gate_out[...] = g_c[...].astype(F32)

    def misc_chain():
        stages = [
            (Swap(mail, m_z, p.z, NZ, z_dev), m_z, p.z),
            (Swap(mail, m_y, p.y, 4, y_dev), m_y, p.y),
            (Swap(mail, m_x, p.x, 4, x_dev), m_x, p.x),
            (Swap(mail, m_c, p.c, 2, c_dev), m_c, p.c),
        ]
        value = misc[...]
        for swap, buf, me in stages:
            buf[me] = value
            swap.start()
            yield
            value = swap.total()
        misc_out[...] = value

    running = [gate_chain(), up_chain(), dn_chain(), misc_chain()]
    while running:
        left = []
        for chain in running:
            try:
                next(chain)
                left.append(chain)
            except StopIteration:
                pass
        running = left
    mail.finish()


def reduce(up, dn, gt, misc):
    vm = lambda *dims: pltpu.VMEM(dims, BF16)
    return pl.pallas_call(
        reduce_kernel,
        name="reduce",
        out_shape=(
            shape((96, HID), F32),
            shape((96, HID), F32),
            shape((2, 96, GATE), F32),
            shape((8, 128), F32),
        ),
        in_specs=[VMEM] * 4,
        out_specs=(VMEM,) * 4,
        scratch_shapes=[
            vm(8, 96, 2 * HID),
            vm(8, 96, 2 * HID),
            vm(D, GATE),
            vm(2, 4, 96, 2 * HID),
            vm(2, 4, 96, 2 * HID),
            vm(D, GATE),
            vm(2, 96, 2 * HID),
            vm(2, 2, 96, 2 * HID),
            vm(2, 48, HID),
            vm(2, 96, HID),
            vm(2, 2, 96, HID),
            vm(2, 4, 96, HID),
            vm(2, 48, HID),
            vm(2, 96, HID),
            vm(4, 3, 96, GATE),
            vm(4, 4, 96, GATE),
            vm(4, 192, GATE),
            vm(8, 96, GATE),
            vm(2, 96, GATE),
            pltpu.VMEM((NZ, 8, 128), F32),
            pltpu.VMEM((4, 8, 128), F32),
            pltpu.VMEM((4, 8, 128), F32),
            pltpu.VMEM((2, 8, 128), F32),
            pltpu.SemaphoreType.DMA((64,)),
            pltpu.SemaphoreType.DMA((64,)),
        ],
        compiler_params=pltpu.CompilerParams(collective_id=3, has_side_effects=True, vmem_limit_bytes=VMEM_LIMIT),
    )(up.reshape(8, 2, 96, 2 * HID), dn.reshape(8, 2, 96, 2 * HID), gt, misc)


def layer_norm(row_block, ln_gain):
    values = row_block.astype(F32)
    center = values - jnp.mean(values, axis=1, keepdims=True)
    spread = jnp.mean(center * center, axis=1, keepdims=True)
    return (center * lax.rsqrt(spread + 1e-06) * ln_gain).astype(BF16)


def gelu_value(preact):
    return 0.5 * preact * (1.0 + lax.erf(preact * 0.7071067811865476))


def gelu_slope(preact):
    return (
        0.5 * (1.0 + lax.erf(preact * 0.7071067811865476))
        + preact * jnp.exp(-0.5 * preact * preact) * 0.3989422804014327
    )


def dot(a, b, dims=((1,), (0,))):
    return lax.dot_general(a, b, (dims, ((), ())), preferred_element_type=F32)


def per_device(
    patch_class_features, live_tiles, tile_patient, ln_gain, up_weight, down_weight, tanh_weight,
    sigmoid_weight, score_weight, queue_keys, queue_labels, patient_labels, loss_scale,
):
    slot = lax.broadcasted_iota(jnp.int32, (ROWS,), 0)
    marker = jnp.where(slot < live_tiles[0], tile_patient, 16)[None, :]
    normed_own = layer_norm(patch_class_features, ln_gain)
    gate_weight = jnp.concatenate([tanh_weight, sigmoid_weight], axis=1)
    normed, up, down, w = gather(normed_own, up_weight, down_weight, gate_weight)

    key_squares = jnp.einsum("kd,kd->k", queue_keys, queue_keys, preferred_element_type=F32)
    keys = (queue_keys * lax.rsqrt(key_squares + 1e-06)[:, None]).astype(BF16)
    preact = dot(normed, up)
    hidden = gelu_value(preact).astype(BF16)
    through = dot(down, w).astype(BF16)
    part = dot(hidden, through).astype(BF16)
    labels = jnp.concatenate([patient_labels, patient_labels])[:, None]
    uv, score_grads, alpha, mass, pooled_grad, misc = head(
        part, patch_class_features, w, hidden, down, keys, queue_labels[None, :], labels, marker,
        score_weight[None, :], loss_scale.reshape(1, 1),
    )

    pre = (score_grads.reshape(TOK, 1) * uv.astype(F32)).astype(BF16)
    weights = jnp.where(mass > 0.0, alpha[:, None, :], 0.0)[:, :4]
    weights = weights.transpose(0, 2, 1).reshape(TOK, 4).astype(BF16)
    grad4 = pooled_grad[:4].astype(BF16)
    grad_hidden = dot(grad4, down, ((1,), (1,))).astype(BF16)
    hidden_grad = dot(pre, through, ((1,), (1,))) + dot(weights, grad_hidden)
    pre_grad = (hidden_grad * gelu_slope(preact)).astype(BF16)
    up_part = dot(normed, pre_grad, ((0,), (0,))).astype(BF16)
    held = dot(pre, hidden, ((0,), (0,))).astype(BF16)
    held4 = dot(weights, hidden, ((0,), (0,))).astype(BF16)
    down_part = (dot(w, held) + dot(grad4, held4, ((0,), (0,)))).astype(BF16)
    z = lax.axis_index("tile") // 2
    pre_own = lax.dynamic_slice_in_dim(pre, z * ROWS, ROWS, 0)
    gate_part = (dot(down, held, ((0,), (1,))) + dot(patch_class_features, pre_own, ((0,), (0,)))).astype(BF16)
    up_grad, down_grad, gate_grad, total = reduce(up_part, down_part, gate_part, misc)
    return (up_grad, down_grad.T, gate_grad[0], gate_grad[1], total[:2].reshape(2 * 128), total[2, 0])


def solution(mesh):
    placed = (
        P(("pat", "tile"), None),
        P(("pat", "tile")),
        P(("pat", "tile")),
        P(),
        P(None, "tile"),
        P("tile", None),
        P("tile", None),
        P("tile", None),
        P(),
        P("tile", None),
        P("tile"),
        P("pat"),
        P(),
    )
    return jax.shard_map(
        per_device,
        mesh=mesh,
        in_specs=placed,
        out_specs=(P("pat", "tile"), P("tile", "pat"), P("tile", None), P("tile", None), P(), P()),
        check_vma=False,
    )
```

time: 1250 us -> 262 us (0.21)
  waiting for transfers between devices: 753 us -> 0 us
  blocking collectives: 399 us -> 0 us
  Pallas kernels: 0 us -> 199 us
  between operations: 17.4 us -> 2.54 us
  matrix products: 49.3 us -> 36.2 us
    reduce_scatter x5 -> x0, waiting for transfers between devices: 516 us -> none  [the longest x1 204 us: per_device(): lax.psum_scatter(jnp.einsum('rd,rl->dl', head_in, sigmoid_pre, preferred_...]
    psum x5 -> x0, blocking collectives: 276 us -> none  [the longest x1 75.3 us: per_device(): lax.psum(jnp.dot(score_derivative_lines, direction_queue_entry, preferred...]
    all_gather x2 -> x0, waiting for transfers between devices: 236 us -> none  [the longest x1 121 us: per_device(): lax.all_gather(patch_class_features, 'tile', axis=0, tiled=True)]
    pallas_call x0 -> x3, Pallas kernels: none -> 199 us  [the longest x1 88.9 us: gather(): pl.pallas_call(gather_kernel, name='gather', out_shape=(shape((TOK, D), B...]
    all_gather x3 -> x0, blocking collectives: 123 us -> none  [the longest x1 44.6 us: per_device(): lax.all_gather(sigmoid_weight, 'tile', axis=0, tiled=True)]
    dot_general x14 -> x11, matrix products: 49.3 us -> 36.2 us  [dot(): return lax.dot_general(a, b, (dims, ((), ())), preferred_element_type=F32)]
  transfers between devices with their start and end apart: 7 -> 0, of which waited for: 7 -> 0; matrix products, arithmetic and copies ran while one was open for 2% -> 0% of each run, Pallas kernels for 0% -> 0%
where the time goes in v1:
time: 262 us; the launch traced here: 259 us
  Pallas kernels  199 us (76%)
  matrix products  36.2 us (14%)
  other arithmetic  13.1 us (5%)
  local copies, waits for them, and re-layouts  8.73 us (3%)
    pallas_call x1, Pallas kernels, gather(): pl.pallas_call(gather_kernel, name='gather', out_shape=(shape((TOK, D), B...  88.9 us
    pallas_call x1, Pallas kernels, head(): pl.pallas_call(head_kernel, name='head', out_shape=(shape((TOK, 2 * GATE)...  68.1 us
    pallas_call x1, Pallas kernels, reduce(): pl.pallas_call(reduce_kernel, name='reduce', out_shape=(shape((96, HID),...  41.7 us
    dot_general x11, matrix products, dot(): return lax.dot_general(a, b, (dims, ((), ())), preferred_element_type=F32)  36.2 us

profile of v1, /device:TPU:32, one launch (start us, length us, event | category | flops | bytes accessed | tf_op | source)
XLA Modules:
  0.0 259.3 jit_solution(3117321872698976836)
XLA Ops:
  3.6 1.3 add_bitcast_fusion
  6.0 1.2 fusion.13
  7.3 1.3 copy.21.plab_ref
  8.6 2.6 fusion.1
  12.9 2.3 fusion.key_ref
  15.2 88.9 %gather.1 = (bf16[1024,1536]{1,0:T(8,128)(2,1)}, bf16[1536,768]{1,0:T(8,128)(2,1)}, bf16[768,1536]{1,0:T(8,128)(2,1)}, bf16[1536,512]{1,0:T(8,128)(2,1)}) custom-call(bf16[128,1536]{1,0:T(8,128)(2,1)} %fusion.15.nm, bf16[1536,384]{1,0:T(8,128)(2,1)} %up.1, bf16[384,1536]{1,0:T(8,128)(2,1)} %dn.1, bf16[96,512]{1,0:T(8,128)(2,1)} %pad_maximum_fusion.wg), custom_call_target="tpu_custom_call" | custom-call | tf_op jit(solution)/shard_map/gather/pallas_call | solution.py:274
  104.1 3.6 %convolution_convert_fusion.3 = bf16[768,512]{1,0:T(8,128)(2,1)S(1)} fusion(bf16[768,1536]{1,0:T(8,128)(2,1)} %get-tuple-element.22.dn_ref, bf16[1536,512]{1,0:T(8,128)(2,1)} %get-tuple-element.23.w_ref), kind=kOutput, calls=%fused_computation.21 | convolution fusion | flops 1208352768 | bytes 4718592 | tf_op jit(solution)/shard_map/dot_general | solution.py:689
  107.9 4.3 %multiply_convert_fusion = (bf16[1024,768]{1,0:T(8,128)(2,1)S(1)}, f32[1024,768]{1,0:T(8,128)}) fusion(bf16[1024,1536]{1,0:T(8,128)(2,1)S(1)} %copy-done.14, bf16[1536,768]{1,0:T(8,128)(2,1)S(1)} %copy-done.15), kind=kOutput, calls=%fused_computation.15 | convolution fusion | flops 2419851264 | bytes 10223616 | tf_op jit(solution)/shard_map/dot_general | solution.py:689
  112.2 2.0 convolution_convert_fusion.1.part
  114.2 68.1 %head.1 = (bf16[1024,512]{1,0:T(8,128)(2,1)}, f32[8,128]{1,0:T(8,128)}, f32[8,128]{1,0:T(8,128)}, f32[8,8,128]{2,1,0:T(8,128)}, f32[8,1536]{1,0:T(8,128)}, /*index=5*/f32[8,128]{1,0:T(8,128)}) custom-call(bf16[1024,512]{1,0:T(8,128)(2,1)} %convolution_convert_fusion.1.part, bf16[128,1536]{1,0:T(8,128)(2,1)} %x_ref.1, ...), custom_call_target="tpu_custom_call" | custom-call | tf_op jit(solution)/shard_map/head/pallas_call | solution.py:441
  182.3 1.6 multiply_convert_fusion.1
  184.0 1.5 convolution_convert_fusion.4
  186.6 1.7 fusion.28
  188.3 1.8 fusion.9.gt
  190.0 2.7 %fusion.27 = f32[1024,768]{1,0:T(8,128)} fusion(bf16[1024,512]{1,0:T(8,128)(2,1)S(1)} %multiply_convert_fusion.1, bf16[768,512]{1,0:T(8,128)(2,1)S(1)} %convolution_convert_fusion.3), kind=kOutput, calls=%fused_computation.51 | convolution fusion | flops 805306368 | bytes 4980736 | tf_op jit(solution)/shard_map/dot_general | solution.py:689
  192.8 9.0 %convolution_convert_fusion = bf16[1536,768]{1,0:T(8,128)(2,1)} fusion(bf16[1024,1536]{1,0:T(8,128)(2,1)} %get-tuple-element.20, f32[1024,768]{1,0:T(8,128)} %get-tuple-element.37, f32[1024,768]{1,0:T(8,128)} %fusion.27, bf16[4,768]{1,0:T(4,128)(2,1)S(1)} %convolution_convert_fusion.4, f32[8,8,128]{2,1,0:T(8,128)S(1)} %copy-done.11, f32[8,128]{1,0:T(8,128)S(1)} %copy-done.13), kind=kOutput, calls=%fused_computation.6 | convolution fusion | flops 2432049152 | bytes 11823104 | tf_op jit(solution)/shard_map/dot_general | solution.py:689
  201.8 3.2 %fusion.10 = f32[1536,768]{1,0:T(8,128)} fusion(bf16[1024,768]{1,0:T(8,128)(2,1)S(1)} %copy-done.6, f32[8,1536]{1,0:T(8,128)S(1)} %copy-done.8, f32[8,8,128]{2,1,0:T(8,128)S(1)} %copy-done.11, f32[8,128]{1,0:T(8,128)S(1)} %copy-done.13), kind=kOutput, calls=%fused_computation.24 | convolution fusion | flops 15739904 | bytes 6324224 | tf_op jit(solution)/shard_map/dot_general | solution.py:689
  205.0 5.4 %add_convert_fusion = bf16[1536,768]{1,0:T(8,128)(2,1)} fusion(f32[1536,768]{1,0:T(8,128)} %fusion.10, bf16[1536,512]{1,0:T(8,128)(2,1)S(1)} %copy-done.4, bf16[512,768]{1,0:T(8,128)(2,1)} %copy-done.7), kind=kOutput, calls=%fused_computation.5 | convolution fusion | flops 1210318848 | bytes 9437184 | tf_op jit(solution)/shard_map/dot_general | solution.py:689
  210.4 41.7 %reduce.3 = (f32[96,384]{1,0:T(8,128)}, f32[96,384]{1,0:T(8,128)}, f32[2,96,256]{2,1,0:T(8,128)}, f32[8,128]{1,0:T(8,128)}) custom-call(bf16[8,2,96,768]{3,2,1,0:T(8,128)(2,1)} %bitcast.55, bf16[8,2,96,768]{3,2,1,0:T(8,128)(2,1)} %bitcast.54, bf16[1536,512]{1,0:T(8,128)(2,1)} %fusion.9.gt, f32[8,128]{1,0:T(8,128)} %get-tuple-element.29.misc), custom_call_target="tpu_custom_call" | custom-call | tf_op jit(solution)/shard_map/reduce/pallas_call | solution.py:628
  252.1 1.2 slice.25
  253.3 1.2 slice_bitcast_fusion.2
  254.5 1.6 slice_bitcast_fusion
  256.2 1.6 copy.32
  257.7 1.6 copy.33
  (40 shorter events, 5.3 us)
Async XLA Ops:
  0.6 11.2 %copy-start.1 = (bf16[128,1536]{1,0:T(8,128)(2,1)S(1)}, bf16[128,1536]{1,0:T(8,128)(2,1)}, u32[]{:S(2)}) copy-start(bf16[128,1536]{1,0:T(8,128)(2,1)} %x_ref.1) | copy-start | bytes 1179652
  0.6 12.2 %copy-start = (bf16[1024,1536]{1,0:T(8,128)(2,1)S(1)}, bf16[1024,1536]{1,0:T(8,128)(2,1)}, u32[]{:S(2)}) copy-start(bf16[1024,1536]{1,0:T(8,128)(2,1)} %param.22) | copy-start | bytes 9437188
  0.7 11.2 %copy-start.12 = (f32[1536]{0:T(1024)S(1)}, f32[1536]{0:T(1024)}, u32[]{:S(2)}) copy-start(f32[1536]{0:T(1024)} %param.16) | copy-start | bytes 18436
  8.6 2.6 copy-start.9
  8.6 2.6 %copy-start.10 = (bf16[96,256]{1,0:T(8,128)(2,1)S(1)}, bf16[96,256]{1,0:T(8,128)(2,1)}, u32[]{:S(2)}) copy-start(bf16[96,256]{1,0:T(8,128)(2,1)} %param.19) | copy-start | bytes 147460
  104.1 3.7 %copy-start.14 = (bf16[1024,1536]{1,0:T(8,128)(2,1)S(1)}, bf16[1024,1536]{1,0:T(8,128)(2,1)}, u32[]{:S(2)}) copy-start(bf16[1024,1536]{1,0:T(8,128)(2,1)} %get-tuple-element.20) | copy-start | bytes 9437188
  104.1 3.8 %copy-start.15 = (bf16[1536,768]{1,0:T(8,128)(2,1)S(1)}, bf16[1536,768]{1,0:T(8,128)(2,1)}, u32[]{:S(2)}) copy-start(bf16[1536,768]{1,0:T(8,128)(2,1)} %get-tuple-element.21) | copy-start | bytes 7077892
  112.2 2.0 copy-start.5
  114.2 69.8 %copy-start.3 = (bf16[768,1536]{1,0:T(8,128)(2,1)S(1)}, bf16[768,1536]{1,0:T(8,128)(2,1)}, u32[]{:S(2)}) copy-start(bf16[768,1536]{1,0:T(8,128)(2,1)} %get-tuple-element.22.dn_ref) | copy-start | bytes 7077892
  182.3 3.1 %copy-start.6 = (bf16[1024,768]{1,0:T(8,128)(2,1)S(1)}, bf16[1024,768]{1,0:T(8,128)(2,1)}, u32[]{:S(2)}) copy-start(bf16[1024,768]{1,0:T(8,128)(2,1)} %copy-done.5) | copy-start | bytes 4718596
  186.6 1.7 copy-start.7
  186.6 1.7 copy-start.2
  190.0 2.7 %copy-start.11 = (f32[8,8,128]{2,1,0:T(8,128)S(1)}, f32[8,8,128]{2,1,0:T(8,128)}, u32[]{:S(2)}) copy-start(f32[8,8,128]{2,1,0:T(8,128)} %get-tuple-element.26) | copy-start | bytes 98308
  190.0 2.7 %copy-start.13 = (f32[8,128]{1,0:T(8,128)S(1)}, f32[8,128]{1,0:T(8,128)}, u32[]{:S(2)}) copy-start(f32[8,128]{1,0:T(8,128)} %get-tuple-element.27) | copy-start | bytes 12292
  192.8 9.0 %copy-start.8 = (f32[8,1536]{1,0:T(8,128)S(1)}, f32[8,1536]{1,0:T(8,128)}, u32[]{:S(2)}) copy-start(f32[8,1536]{1,0:T(8,128)} %get-tuple-element.28) | copy-start | bytes 147460
  201.8 3.2 %copy-start.4 = (bf16[1536,512]{1,0:T(8,128)(2,1)S(1)}, bf16[1536,512]{1,0:T(8,128)(2,1)}, u32[]{:S(2)}) copy-start(bf16[1536,512]{1,0:T(8,128)(2,1)} %get-tuple-element.23.w_ref) | copy-start | bytes 4718596

commit v2 on v0

v2 whole, which is shorter than its diff:
```python
import jax
import jax.numpy as jnp
from jax import lax
from jax.experimental import pallas as pl
from jax.experimental.pallas import tpu as pltpu
from jax.sharding import PartitionSpec as P

MESH = pl.DeviceIdType.MESH
F32 = jnp.float32
BF16 = jnp.bfloat16
HIGH = lax.Precision.HIGHEST
INV_TEMP = 1.0 / 0.07
NZ = 8
NY = 4
NX = 4
ROWS = 128
TOK = NZ * ROWS
D = 1536
HID = 384
GATE = 256
VMEM_LIMIT = 63 << 20


class Place:
    def __init__(self):
        self.pat = lax.axis_index("pat")
        self.tile = lax.axis_index("tile")
        self.z = lax.div(self.tile, 2)
        self.q = lax.rem(self.tile, 2)
        self.xl = lax.div(self.pat, 8)
        self.y = lax.rem(lax.div(self.pat, 2), 4)
        self.c = lax.rem(self.pat, 2)
        self.x = self.q * 2 + self.xl

    def at(self, z=None, y=None, x=None, c=None):
        z = self.z if z is None else z
        y = self.y if y is None else y
        c = self.c if c is None else c
        if x is None:
            xl, q = self.xl, self.q
        else:
            xl, q = lax.rem(x, 2), lax.div(x, 2)
        return (xl * 8 + y * 2 + c, z * 2 + q)

    def dz(self, d):
        return lax.rem(self.z + (d + NZ), NZ)

    def dy(self, d):
        return lax.rem(self.y + (d + NY), NY)

    def dx(self, d):
        return lax.rem(self.x + (d + NX), NX)


def dot(a, b, dims=((1,), (0,))):
    return lax.dot_general(a, b, (dims, ((), ())), preferred_element_type=F32)


class Mail:
    def __init__(self, send_sem, recv_sem):
        self.send_sem, self.recv_sem = send_sem, recv_sem
        self.next = 0
        self.sent = []

    def slots(self, n):
        first = self.next
        self.next += n
        return first

    def send(self, k, src, dst, device):
        copy = pltpu.make_async_remote_copy(
            src_ref=src, dst_ref=dst, send_sem=self.send_sem.at[k], recv_sem=self.recv_sem.at[k],
            device_id=device, device_id_type=MESH,
        )
        copy.start()
        self.sent.append(copy)

    def arrive(self, k, dst, device):
        pltpu.make_async_remote_copy(
            src_ref=dst, dst_ref=dst, send_sem=self.send_sem.at[k], recv_sem=self.recv_sem.at[k],
            device_id=device, device_id_type=MESH,
        ).wait_recv()

    def finish(self):
        for copy in self.sent:
            copy.wait_send()


def rows_at(index, size, offset=0, count=None):
    count = size if count is None else count
    return pl.ds(pl.multiple_of(index * size + offset, 16), count)


def lanes_at(index, size):
    return pl.ds(pl.multiple_of(index * size, 128), size)


class ZGather:
    def __init__(self, mail, place, ref, size):
        self.mail, self.place, self.ref, self.size = mail, place, ref, size
        self.half = size // 2
        self.key = mail.slots(16)
        self.chains = ((1, 0, 4), (-1, 0, 3), (1, 1, 3), (-1, 1, 4))

    def piece(self, owner, half):
        return self.ref.at[rows_at(owner, self.size, half * self.half, self.half)]

    def step(self, s, which=(0, 1, 2, 3)):
        p = self.place
        for i in which:
            way, half, steps = self.chains[i]
            block = self.piece(p.dz(-way * s), half)
            if 0 < s <= steps:
                self.mail.arrive(self.key + i * 4 + s - 1, block, p.at(z=p.dz(-way)))
            if s < steps:
                self.mail.send(self.key + i * 4 + s, block, block, p.at(z=p.dz(way)))


class ZReduce:
    def __init__(self, mail, place, ref, size, stage, recv):
        self.mail, self.place, self.ref, self.size = mail, place, ref, size
        self.stage, self.recv = stage, recv
        self.half = size // 2
        self.key = mail.slots(16)
        self.chains = ((1, 0, 4), (-1, 1, 4), (1, 1, 3), (-1, 0, 3))

    def piece(self, owner, half):
        return rows_at(owner, self.size, half * self.half, self.half)

    def step(self, s):
        p = self.place
        for i, (way, half, steps) in enumerate(self.chains):
            if s < steps:
                dest = self.piece(p.dz(way * (steps - s)), half)
                if s == 0:
                    src = self.ref.at[dest]
                else:
                    self.mail.arrive(self.key + i * 4 + s - 1, self.recv.at[i, s - 1], p.at(z=p.dz(-way)))
                    src = self.stage.at[i, s - 1]
                    src[...] = (self.ref[dest].astype(F32) + self.recv[i, s - 1].astype(F32)).astype(BF16)
                self.mail.send(self.key + i * 4 + s, src, self.recv.at[i, s], p.at(z=p.dz(way)))

    def total(self):
        p = self.place
        for i, (way, half, steps) in enumerate(self.chains):
            self.mail.arrive(self.key + i * 4 + steps - 1, self.recv.at[i, steps - 1], p.at(z=p.dz(-way)))
        first = self.ref[self.piece(p.z, 0)].astype(F32) + self.recv[0, 3].astype(F32) + self.recv[3, 2].astype(F32)
        second = self.ref[self.piece(p.z, 1)].astype(F32) + self.recv[1, 3].astype(F32) + self.recv[2, 2].astype(F32)
        return jnp.concatenate([first, second], axis=0)


class Swap:
    def __init__(self, mail, ref, me, n, device_of):
        self.mail, self.ref, self.me, self.n, self.device_of = mail, ref, me, n, device_of
        self.key = mail.slots(n - 1)

    def other(self, d):
        return lax.rem(self.me + d, self.n)

    def start(self):
        for d in range(1, self.n):
            mine = self.ref.at[self.me]
            self.mail.send(self.key + d - 1, mine, mine, self.device_of(self.other(d)))

    def wait(self):
        for d in range(1, self.n):
            source = self.other(self.n - d)
            self.mail.arrive(self.key + d - 1, self.ref.at[source], self.device_of(source))

    def total(self):
        self.wait()
        value = self.ref[0].astype(F32)
        for j in range(1, self.n):
            value = value + self.ref[j].astype(F32)
        return value


def two_part(a):
    top = a.astype(BF16).astype(F32)
    return jnp.concatenate([top, a - top], axis=0).astype(BF16)


def dot_two(a, b, transposed=False):
    dims = (((1,), (1,)), ((), ())) if transposed else (((1,), (0,)), ((), ()))
    both = lax.dot_general(two_part(a), b, dims, preferred_element_type=F32)
    half = a.shape[0]
    return both[:half] + both[half:]


def add_into(acc, others):
    value = acc[...].astype(F32)
    for other in others:
        value = value + other[...].astype(F32)
    acc[...] = value.astype(BF16)


def ring_sum(mail, key, pos, nxt, prv, get, half, hbuf, fbuf):
    at = lambda d: lax.rem(pos + d, 4)
    mail.send(key, half(get(at(2)), 0), hbuf.at[0], nxt)
    mail.send(key + 1, half(get(at(2)), 1), hbuf.at[1], prv)
    yield
    mail.arrive(key, hbuf.at[0], prv)
    add_into(half(get(at(1)), 0), [hbuf.at[0]])
    mail.send(key + 2, get(at(1)), fbuf.at[0], nxt)
    mail.arrive(key + 1, hbuf.at[1], nxt)
    add_into(half(get(at(3)), 1), [hbuf.at[1]])
    mail.send(key + 3, get(at(3)), fbuf.at[1], prv)
    yield
    mail.arrive(key + 2, fbuf.at[0], prv)
    mail.arrive(key + 3, fbuf.at[1], nxt)


K_GELU = 0.7071067811865476
K_SLOPE = 0.3989422804014327
BLOCK16 = 16


def gelu_rows(pre_t, h_s, slope_s, t, row, lanes):
    v = pre_t[pl.ds(t, BLOCK16)]
    half = 0.5 * (1.0 + lax.erf(v * K_GELU))
    h_s[pl.ds(row, BLOCK16), lanes] = (v * half).astype(BF16)
    slope_s[pl.ds(row, BLOCK16), lanes] = (half + v * jnp.exp(-0.5 * v * v) * K_SLOPE).astype(BF16)


def kernel(
    x_ref, live, tile_patient, gain, up_hbm, dn_hbm, wt, ws, sw_ref, keys_hbm, qlab, plab, scale,
    up_out, dn_out, gate_out, misc_out,
    n_all, n_t, x_t, up_b, dn_b, dn_t, wq, w_x, thru, thru_t, h_s, h_t, slope_s, part, uv_all, keys, keys_t,
    pg_s, pre_s, held_t, held, pre_t,
    stage, recv, pbuf, zbuf, xbuf, sbuf, score_all, alpha_all, col_t,
    gt_p, up0, dn0, gt0, up_acc, dn_acc, g_acc, u_yh, u_yf, u_xh, u_xf, d_xh, d_xf, d_yh, d_yf,
    g_stage, g_recv, g_y, g_x, g_c, m_z, m_y, m_x, m_c,
    send_sem, recv_sem, local_sem,
):
    p = Place()
    mail = Mail(send_sem, recv_sem)
    mate, beside = p.at(c=1 - p.c), p.at(x=3 - p.x)
    above, below = p.at(y=p.dy(1)), p.at(y=p.dy(-1))
    z_dev = lambda z: p.at(z=z)
    y_dev = lambda y: p.at(y=y)
    x_dev = lambda x: p.at(x=x)
    c_dev = lambda c: p.at(c=c)
    q_dev = lambda q: (p.pat, p.z * 2 + q)
    partners = (
        [z_dev(p.dz(d)) for d in range(1, NZ)]
        + [y_dev(p.dy(d)) for d in (1, 2, 3)]
        + [x_dev(p.dx(d)) for d in (1, 2, 3)]
        + [mate]
    )
    barrier = pltpu.get_barrier_semaphore()
    for device in partners:
        pl.semaphore_signal(barrier, inc=1, device_id=device, device_id_type=MESH)

    fetch_up = pltpu.make_async_copy(up_hbm, up_b.at[p.q], local_sem.at[0])
    fetch_dn = pltpu.make_async_copy(dn_hbm, dn_b.at[p.q], local_sem.at[1])
    fetch_keys = pltpu.make_async_copy(keys_hbm, keys, local_sem.at[2])
    fetch_up.start()
    fetch_dn.start()
    fetch_keys.start()

    def norm_rows(i, carry):
        v = x_ref[pl.ds(pl.multiple_of(i * BLOCK16, BLOCK16), BLOCK16)].astype(F32)
        center = v - jnp.mean(v, axis=1, keepdims=True)
        spread = jnp.mean(center * center, axis=1, keepdims=True)
        n_all[pl.ds(pl.multiple_of(p.z * ROWS + i * BLOCK16, BLOCK16), BLOCK16)] = (
            center * lax.rsqrt(spread + 1e-06) * gain[...]
        ).astype(BF16)
        return carry

    g_rows = pl.ds(pl.multiple_of(p.c * 48, 16), 48)
    g_lanes = lanes_at(lax.rem(p.y, 2), 128)
    wq[p.c, p.y, p.z, p.q] = jnp.where(p.y < 2, wt[g_rows, g_lanes], ws[g_rows, g_lanes])

    lax.fori_loop(0, 4, norm_rows, 0)
    pl.semaphore_wait(barrier, len(partners))

    tokens = ZGather(mail, p, n_all, ROWS)
    k_w = mail.slots(1)
    own_w = wq.at[p.c, p.y, p.z, p.q]
    mail.send(k_w, own_w, own_w, beside)
    tokens.step(0, (0, 1))
    lax.fori_loop(4, 8, norm_rows, 0)
    tokens.step(0, (2, 3))

    k_half = mail.slots(2)
    up_half = lambda q, c: up_b.at[q, rows_at(c, 768)]
    dn_half = lambda q, c: dn_b.at[q, rows_at(c, 192)]
    fetch_up.wait()
    mail.send(k_half, up_half(p.q, p.c), up_half(p.q, p.c), beside)
    fetch_dn.wait()
    mail.send(k_half + 1, dn_half(p.q, p.c), dn_half(p.q, p.c), beside)

    def hidden(owners, q):
        lhs = jnp.concatenate([n_all[rows_at(o, ROWS)] for o in owners], axis=0)
        count = len(owners) * ROWS
        pre_t[pl.ds(0, count)] = dot(lhs, up_b[q])
        lanes = lanes_at(q, HID)
        for j, o in enumerate(owners):
            def body(i, carry, j=j, o=o):
                t = pl.multiple_of(j * ROWS + i * BLOCK16, BLOCK16)
                row = pl.multiple_of(o * ROWS + i * BLOCK16, BLOCK16)
                gelu_rows(pre_t, h_s, slope_s, t, row, lanes)
                return carry

            lax.fori_loop(0, ROWS // BLOCK16, body, 0)

    def turn(owners):
        for o in owners:
            n_t[:, lanes_at(o, ROWS)] = n_all[rows_at(o, ROWS)].T

    k_wz = mail.slots(7)
    w_z = lambda z: wq.at[p.c, p.y, z]

    def w_step(s):
        for way, steps, key in ((1, 4, k_wz), (-1, 3, k_wz + 4)):
            block = w_z(p.dz(-way * s))
            if 0 < s <= steps:
                mail.arrive(key + s - 1, block, z_dev(p.dz(-way)))
            if s < steps:
                mail.send(key + s, block, block, z_dev(p.dz(way)))

    mail.arrive(k_w, wq.at[p.c, p.y, p.z, 1 - p.q], beside)
    w_step(0)
    hidden([p.z], p.q)
    turn([p.z])
    x_t[...] = x_ref[...].T
    w_step(1)
    tokens.step(1, (0, 1))
    tokens.step(1, (2, 3))
    w_step(2)
    near = [p.dz(1), p.dz(-1)]
    hidden(near, p.q)
    turn(near)
    w_step(3)
    fetch_keys.wait()

    def key_rows(i, carry):
        at = pl.ds(pl.multiple_of(i * BLOCK16, BLOCK16), BLOCK16)
        v = keys[at].astype(F32)
        keys[at] = (v * lax.rsqrt(jnp.sum(v * v, axis=1, keepdims=True) + 1e-06)).astype(BF16)
        return carry

    lax.fori_loop(0, 32, key_rows, 0)
    w_step(4)
    k_wy = mail.slots(4)
    w_y = lambda y: wq.at[p.c, y]
    w_yh = lambda y, half: wq.at[p.c, y, pl.ds(half * 4, 4)]
    mail.send(k_wy, w_y(p.y), w_y(p.y), above)
    mail.send(k_wy + 1, w_y(p.y), w_y(p.y), below)
    tokens.step(2, (0, 1))
    theirs, other = 1 - p.q, 1 - p.c
    k_mate = mail.slots(3)
    mail.arrive(k_half, up_half(theirs, p.c), beside)
    mail.send(k_mate, up_half(theirs, p.c), up_half(theirs, p.c), mate)
    tokens.step(2, (2, 3))
    lax.fori_loop(32, 64, key_rows, 0)
    mid = [p.dz(2), p.dz(-2)]
    hidden(mid, p.q)
    turn(mid)
    mail.arrive(k_wy, w_y(p.dy(-1)), below)
    mail.send(k_wy + 2, w_yh(p.dy(-1), 0), w_yh(p.dy(-1), 0), above)
    mail.arrive(k_wy + 1, w_y(p.dy(1)), above)
    mail.send(k_wy + 3, w_yh(p.dy(1), 1), w_yh(p.dy(1), 1), below)
    mail.arrive(k_mate, up_half(theirs, other), mate)
    hidden([p.z], theirs)
    hidden(near, theirs)
    tokens.step(3, (0, 1))
    mail.arrive(k_wy + 2, w_yh(p.dy(2), 0), below)
    mail.arrive(k_wy + 3, w_yh(p.dy(2), 1), above)
    mail.send(k_mate + 2, wq.at[p.c], wq.at[p.c], mate)
    tokens.step(3, (2, 3))
    for j in range(2):
        keys_t[:, pl.ds(j * 512, 512)] = keys[pl.ds(j * 512, 512)].T
    hidden(mid, theirs)
    far = [p.dz(3), p.dz(-3)]
    hidden(far, p.q)
    mail.arrive(k_half + 1, dn_half(theirs, p.c), beside)
    mail.send(k_mate + 1, dn_half(theirs, p.c), dn_half(theirs, p.c), mate)
    hidden(far, theirs)
    turn(far)
    mail.arrive(k_mate + 2, wq.at[other], mate)

    def place_w(t, carry):
        for y in range(4):
            for c in range(2):
                row = pl.multiple_of(t * 96 + c * 48, 16)
                w_x[pl.ds(row, 48), pl.ds(y * 128, 128)] = wq[c, y, lax.div(t, 2), lax.rem(t, 2)]
        return carry

    lax.fori_loop(0, 16, place_w, 0)
    w_full = lambda: w_x[:, pl.ds(0, 2 * GATE)]
    mail.arrive(k_mate + 1, dn_half(theirs, other), mate)
    for q in range(2):
        thru[pl.ds(q * HID, HID)] = dot(dn_b[q], w_full()).astype(BF16)

    def gate_part(o, carry):
        at = rows_at(o, ROWS)
        part[at] = dot(h_s[at], thru[...]).astype(BF16)
        return carry

    lax.fori_loop(0, NZ - 1, lambda d, carry: gate_part(lax.rem(p.z + 5 + d, NZ), carry), 0)
    tokens.step(4)
    last = p.dz(4)
    hidden([last], 0)
    hidden([last], 1)
    gate_part(last, 0)

    reduce = ZReduce(mail, p, part, ROWS, stage, recv)
    gather_uv = ZGather(mail, p, uv_all, ROWS)
    swap_p = Swap(mail, pbuf, p.z, NZ, z_dev)
    swap_z = [Swap(mail, zbuf.at[i], p.z, NZ, z_dev) for i in range(3)]
    swap_x = [Swap(mail, xbuf.at[i], p.q, 2, q_dev) for i in range(3)]
    swap_s = Swap(mail, sbuf, p.z, NZ, z_dev)

    row8 = lax.broadcasted_iota(jnp.int32, (8, 128), 0)
    first4 = row8 < 4
    row_patient = lax.rem(row8, 4)
    first4_wide = lax.broadcasted_iota(jnp.int32, (8, 768), 0) < 4
    lane = lax.broadcasted_iota(jnp.int32, (8, 128), 1)

    def pack(v):
        return jnp.where(first4_wide, v[:, :768], v[:, 768:])

    def unpack(v):
        rolled = pltpu.roll(v, 4, 0)
        return jnp.concatenate([jnp.where(first4_wide, v, rolled), jnp.where(first4_wide, rolled, v)], axis=1)

    reduce.step(0)
    turn([last])
    for q in range(2):
        dn_t[:, pl.ds(q * HID, HID)] = dn_b[q].T
    gate_x = dot(x_ref[...], w_full())
    reduce.step(1)
    same = jnp.zeros((8, 1024), jnp.int32)
    row_wide = lax.rem(lax.broadcasted_iota(jnp.int32, (8, 1024), 0), 4)
    labels = jnp.broadcast_to(qlab[...], (8, 1024))
    for k in range(4):
        same = jnp.where((row_wide == k) & (labels == plab[k]), 1, same)
    same = same.astype(F32)
    label_sums = dot(same.astype(BF16), keys[...])
    positives = jnp.sum(same, axis=1, keepdims=True)
    reduce.step(2)
    for z in range(NZ):
        h_t[:, pl.ds(z * ROWS, ROWS)] = h_s[pl.ds(z * ROWS, ROWS)].T
    reduce.step(3)
    gates = reduce.total() + gate_x
    tanh_val = jnp.tanh(gates[:, :GATE])
    sigmoid_val = jax.nn.sigmoid(gates[:, GATE:])
    product = tanh_val * sigmoid_val
    sw = sw_ref[...]
    score = lax.dot_general(
        jnp.broadcast_to(sw, (8, GATE)), product, (((1,), (1,)), ((), ())), precision=HIGH, preferred_element_type=F32
    )
    in_tile = lax.broadcasted_iota(jnp.int32, (8, 128), 1) < live[0]
    onehot = (jnp.broadcast_to(tile_patient[...], (8, 128)) == row_patient) & in_tile
    mass = jnp.where(onehot, jnp.exp(score), 0.0)
    pbuf[p.z] = mass
    swap_p.start()
    common = sw * sigmoid_val
    own_rows = rows_at(p.z, ROWS)
    uv_all[own_rows, pl.ds(0, GATE)] = (common * (1.0 - tanh_val * tanh_val)).astype(BF16)
    uv_all[own_rows, pl.ds(GATE, GATE)] = (common * tanh_val * (1.0 - sigmoid_val)).astype(BF16)
    gather_uv.step(0)
    vec_x = dot_two(mass, x_ref[...])
    swap_p.wait()

    total = jnp.zeros((8, 1), F32)
    for z in range(NZ):
        total += jnp.sum(pbuf[z], axis=1, keepdims=True)
    mass_all = jnp.concatenate([pbuf[z] for z in range(NZ)], axis=1)
    mass_h = dot_two(mass_all, h_s[...])
    vec = dot_two(mass_h[:, :HID], dn_b[0]) + dot_two(mass_h[:, HID:], dn_b[1]) + vec_x

    def post(i, packed, small):
        zbuf[i, p.z, :, pl.ds(0, 768)] = packed
        zbuf[i, p.z, :, pl.ds(768, 128)] = small
        swap_z[i].start()

    def collect_z(i):
        xbuf[i, p.q] = swap_z[i].total()
        swap_x[i].start()

    post(0, pack(vec), jnp.broadcast_to(total, (8, 128)))
    gather_uv.step(1)
    collect_z(0)
    post(1, pack(label_sums), jnp.broadcast_to(positives, (8, 128)))
    summed = swap_x[0].total()
    total_mass = summed[:, 768:769]
    pooled = unpack(summed[:, :768]) / total_mass
    length = jnp.sqrt(jnp.sum(pooled * pooled, axis=1, keepdims=True) + 1e-06)
    unit = pooled / length

    logits = dot(unit.astype(BF16), keys_t[...]) / 0.07
    exps = jnp.exp(logits)
    exp_part = jnp.sum(exps, axis=1, keepdims=True)
    pos_part = jnp.sum(same * logits, axis=1, keepdims=True)
    post(2, pack(dot_two(exps, keys[...])), jnp.where(lane == 0, exp_part, pos_part))
    gather_uv.step(2)
    collect_z(1)
    thru_t[...] = thru[...].T
    gather_uv.step(3)
    collect_z(2)
    gather_uv.step(4)

    def scaled(b, carry):
        at = rows_at(b, ROWS)
        pre_t[pl.ds(0, ROWS)] = dot(uv_all[at], thru_t[:, pl.ds(0, HID)])
        pre_t[pl.ds(ROWS, ROWS)] = dot(uv_all[at], thru_t[:, pl.ds(HID, HID)])

        def body(i, inner):
            t = pl.multiple_of(i * BLOCK16, BLOCK16)
            row = pl.ds(pl.multiple_of(b * ROWS + t, BLOCK16), BLOCK16)
            for q in range(2):
                lanes = pl.ds(q * HID, HID)
                v = pre_t[pl.ds(pl.multiple_of(q * ROWS + t, BLOCK16), BLOCK16)]
                pg_s[row, lanes] = (v * slope_s[row, lanes].astype(F32)).astype(BF16)
            return inner

        lax.fori_loop(0, ROWS // BLOCK16, body, 0)
        return carry

    labels_total = swap_x[1].total()
    pos_count = labels_total[:, 768:769]
    queue_total = swap_x[2].total()
    exp_total = queue_total[:, 768:769]
    pos_logits = queue_total[:, 769:770]
    unit_grad = (scale[0] * INV_TEMP) * (
        unpack(queue_total[:, :768]) / exp_total - unpack(labels_total[:, :768]) / pos_count
    )
    pooled_grad = (unit_grad - unit * jnp.sum(unit * unit_grad, axis=1, keepdims=True)) / length

    grad_h = dot_two(pooled_grad, dn_t[...])
    own_dots = dot_two(pooled_grad, x_t[...])
    dots = dot_two(grad_h, h_t[...])
    for z in range(NZ):
        block = dots[:, z * ROWS : (z + 1) * ROWS] + jnp.where(p.z == z, own_dots, 0.0)
        picked = jnp.where((pbuf[z] > 0.0) & first4, block, 0.0)
        sbuf[p.z, pl.ds(z, 1)] = jnp.sum(picked, axis=0, keepdims=True)
    swap_s.start()
    center = jnp.sum(pooled * pooled_grad, axis=1, keepdims=True)
    log_part = jnp.log(exp_total) - pos_logits / pos_count
    loss = jnp.sum(jnp.where(first4, jnp.broadcast_to(log_part, (8, 128)), 0.0), axis=0, keepdims=True)
    for z in range(NZ):
        block = jnp.where(first4, pbuf[z], 0.0)
        alpha_all[pl.ds(z, 1)] = jnp.sum(block / total_mass, axis=0, keepdims=True)
        score_all[pl.ds(z, 1)] = jnp.sum(jnp.where(block > 0.0, center, 0.0), axis=0, keepdims=True)
    lax.fori_loop(0, NZ, scaled, 0)
    pad = jnp.zeros((120, 768), F32)
    grad_h_pad = jnp.concatenate([jnp.where(first4_wide, grad_h, 0.0), pad], axis=0).astype(BF16)
    grad_pad = jnp.concatenate([pooled_grad, jnp.zeros((120, D), F32)], axis=0)
    for j in range(D // 128):
        w_x[pl.ds(j * 128, 128), pl.ds(512, 128)] = grad_pad[:, j * 128 : (j + 1) * 128].T.astype(BF16)
    score_all[...] = alpha_all[...] * (swap_s.total() - score_all[...])

    def columns(b, carry):
        mass_b = jnp.where(first4, pbuf[b], 0.0)
        weight = jnp.where(mass_b > 0.0, jnp.broadcast_to(alpha_all[pl.ds(b, 1)], (8, 128)), 0.0)
        grad = jnp.broadcast_to(score_all[pl.ds(b, 1)], (8, 128))
        turned = jnp.concatenate([weight, grad, jnp.zeros((112, 128), F32)], axis=0).T
        col_t[...] = turned
        at = rows_at(b, ROWS)
        both = dot(turned.astype(BF16), grad_h_pad)
        pre_t[pl.ds(0, ROWS)] = both[:, :HID]
        pre_t[pl.ds(ROWS, ROWS)] = both[:, HID:]

        def body(i, inner):
            t = pl.multiple_of(i * BLOCK16, BLOCK16)
            row = pl.ds(pl.multiple_of(b * ROWS + t, BLOCK16), BLOCK16)
            s = col_t[pl.ds(t, BLOCK16)][:, 8:9]
            pre_s[row] = (s * uv_all[row].astype(F32)).astype(BF16)
            for q in range(2):
                lanes = pl.ds(q * HID, HID)
                v = pre_t[pl.ds(pl.multiple_of(q * ROWS + t, BLOCK16), BLOCK16)]
                pg_s[row, lanes] = (
                    s * pg_s[row, lanes].astype(F32) + v * slope_s[row, lanes].astype(F32)
                ).astype(BF16)
            return inner

        lax.fori_loop(0, ROWS // BLOCK16, body, 0)
        return carry + dot_two(weight, h_s[at])

    held4 = lax.fori_loop(0, NZ, columns, jnp.zeros((8, 768), F32))
    score_part = lax.dot_general(
        jnp.broadcast_to(score_all[pl.ds(p.z, 1)], (8, ROWS)), product, (((1,), (0,)), ((), ())),
        precision=HIGH, preferred_element_type=F32,
    )
    misc = jnp.where(
        row8 == 0, score_part[:, :128], jnp.where(row8 == 1, score_part[:, 128:], jnp.where(row8 == 2, loss / 16.0, 0.0))
    )

    def misc_chain(value):
        stages = [
            (Swap(mail, m_z, p.z, NZ, z_dev), m_z, p.z),
            (Swap(mail, m_y, p.y, 4, y_dev), m_y, p.y),
            (Swap(mail, m_x, p.x, 4, x_dev), m_x, p.x),
            (Swap(mail, m_c, p.c, 2, c_dev), m_c, p.c),
        ]
        for swap, buf, me in stages:
            buf[me] = value
            swap.start()
            yield
            value = swap.total()
        misc_out[...] = value
        yield

    misc_steps = misc_chain(misc)
    next(misc_steps)

    for j in range(3):
        held_t[pl.ds(j * 256, 256)] = dot(h_t[pl.ds(j * 256, 256)], pre_s[...]).astype(BF16)

    def gate_rows(i, carry):
        at = pl.ds(pl.multiple_of(i * 256, 256), 256)
        gt_p[at] = (dot(dn_t[at], held_t[...]) + dot(x_t[at], pre_s[own_rows])).astype(BF16)
        return carry

    lax.fori_loop(0, 6, gate_rows, 0)
    k_gt = mail.slots(1)
    mail.send(k_gt, gt_p.at[:, lanes_at(other, GATE)], gt0, mate)
    held[pl.ds(0, 512)] = held_t[...].T
    held[pl.ds(512, 128)] = jnp.concatenate([jnp.where(first4_wide, held4, 0.0), pad], axis=0).astype(BF16)

    up_p = lambda i, c: keys_t.at[pl.ds(pl.multiple_of((i * 2 + c) * 96, 96), 96), pl.ds(0, 768)]
    dn_p = lambda i, c: keys.at[
        pl.ds(pl.multiple_of((lax.rem(i, 4) * 2 + c) * 96, 96), 96), lanes_at(lax.div(i, 4), 768)
    ]
    k_up0, k_dn0 = mail.slots(8), mail.slots(8)

    def compute(block, lhs, rhs, index, k, buf):
        def body(j, carry):
            i = index(j)
            value = dot(lhs[pl.ds(pl.multiple_of(i * 192, 192), 192)], rhs[...]).astype(BF16)
            block(i, 0)[...] = value[:96]
            block(i, 1)[...] = value[96:]
            return carry

        lax.fori_loop(0, 2, body, 0)
        for j in range(2):
            mail.send(k + j, block(index(j), other), buf.at[index(j)], mate)

    def collect(block, index, k, buf, acc):
        for j in range(2):
            mail.arrive(k + j, buf.at[index(j)], mate)

        def body(j, carry):
            i = index(j)
            acc[lax.div(i, 4), lax.rem(i, 4)] = (block(i, p.c)[...].astype(F32) + buf[i].astype(F32)).astype(BF16)
            return carry

        lax.fori_loop(0, 2, body, 0)

    up_index = [lambda j, d=d: j * 4 + p.dy(d) for d in (2, 1, -1, 0)]
    dn_index = [lambda j, x=x, h=h: x * 4 + h * 2 + j for x in (p.xl, 1 - p.xl) for h in (0, 1)]
    up_go = lambda g: compute(up_p, n_t, pg_s, up_index[g], k_up0 + 2 * g, up0)
    up_take = lambda g: collect(up_p, up_index[g], k_up0 + 2 * g, up0, up_acc)
    dn_go = lambda g: compute(dn_p, w_x, held, dn_index[g], k_dn0 + 2 * g, dn0)
    dn_take = lambda g: collect(dn_p, dn_index[g], k_dn0 + 2 * g, dn0, dn_acc)
    rows_half = lambda ref, i: ref.at[pl.ds(i * 48, 48)]
    k_up, k_dn = mail.slots(8), mail.slots(8)
    up_chunk = lambda d: up_acc.at[lax.rem(d, 2), p.y, :, lanes_at(lax.div(d, 2), HID)]
    dn_chunk_x = lambda d: dn_acc.at[lax.rem(d, 2), :, :, lanes_at(lax.div(d, 2), HID)]
    dn_chunk = lambda d: dn_acc.at[p.xl, d, :, lanes_at(p.q, HID)]
    up_y = ring_sum(
        mail, k_up, p.y, above, below, lambda d: up_acc.at[:, d], lambda ref, i: ref.at[i], u_yh, u_yf
    )
    up_x = ring_sum(mail, k_up + 4, p.x, x_dev(p.dx(1)), x_dev(p.dx(-1)), up_chunk, rows_half, u_xh, u_xf)
    dn_x = ring_sum(
        mail, k_dn, p.x, x_dev(p.dx(1)), x_dev(p.dx(-1)), dn_chunk_x, lambda ref, i: ref.at[pl.ds(i * 2, 2)], d_xh, d_xf
    )
    dn_y = ring_sum(mail, k_dn + 4, p.y, above, below, dn_chunk, rows_half, d_yh, d_yf)
    step = lambda chain: next(chain, None)
    zred = ZReduce(mail, p, g_acc, 192, g_stage, g_recv)
    in_y = Swap(mail, g_y, p.y, 4, y_dev)
    k_x = mail.slots(3)
    in_c = Swap(mail, g_c, p.c, 2, c_dev)

    up_go(0)
    mail.arrive(k_gt, gt0, mate)
    g_acc[...] = (gt_p[:, lanes_at(p.c, GATE)].astype(F32) + gt0[...].astype(F32)).astype(BF16)
    zred.step(0)
    up_go(1)
    up_take(0)
    step(up_y)
    step(misc_steps)
    zred.step(1)
    up_go(2)
    dn_go(0)
    zred.step(2)
    dn_go(1)
    up_take(1)
    up_take(2)
    step(up_y)
    dn_take(0)
    dn_take(1)
    step(dn_x)
    zred.step(3)
    step(misc_steps)
    dn_go(2)
    dn_go(3)
    up_go(3)
    g_y[p.y] = zred.total().astype(BF16)
    in_y.start()
    dn_take(2)
    dn_take(3)
    step(dn_x)
    up_take(3)
    step(misc_steps)
    step(up_y)
    add_into(up_acc.at[:, p.y], [u_yf.at[0], u_yf.at[1]])
    step(up_x)
    in_y.wait()

    def row_sum(q):
        rows = pl.ds(pl.multiple_of(q * 96, 96), 96)
        value = g_y[0, rows].astype(F32)
        for j in range(1, 4):
            value = value + g_y[j, rows].astype(F32)
        return value.astype(BF16)

    for d in (1, 2, 3):
        there = p.dx(d)
        g_x[4 + d] = row_sum(lax.div(there, 2))
        mail.send(k_x + d - 1, g_x.at[4 + d], g_x.at[d], x_dev(there))
    g_x[0] = row_sum(p.q)
    step(dn_x)
    add_into(dn_chunk_x(p.x), [d_xf.at[0], d_xf.at[1]])
    step(dn_y)
    step(up_x)
    step(misc_steps)
    for d in (1, 2, 3):
        mail.arrive(k_x + d - 1, g_x.at[d], x_dev(p.dx(-d)))
    value = g_x[0].astype(F32)
    for d in (1, 2, 3):
        value = value + g_x[d].astype(F32)
    g_c[p.c] = value.astype(BF16)
    in_c.start()
    step(dn_y)
    step(up_x)
    up_out[...] = up_chunk(p.x)[...].astype(F32) + u_xf[0].astype(F32) + u_xf[1].astype(F32)
    in_c.wait()
    gate_out[...] = g_c[...].astype(F32)
    step(dn_y)
    dn_out[...] = (dn_chunk(p.y)[...].astype(F32) + d_yf[0].astype(F32) + d_yf[1].astype(F32)).T
    mail.finish()


ANY = pl.BlockSpec(memory_space=pl.ANY)
VMEM = pl.BlockSpec(memory_space=pltpu.VMEM)
SMEM = pl.BlockSpec(memory_space=pltpu.SMEM)


def per_device(
    patch_class_features, live_tiles, tile_patient, ln_gain, up_weight, down_weight, tanh_weight,
    sigmoid_weight, score_weight, queue_keys, queue_labels, patient_labels, loss_scale,
):
    out = lambda *dims: jax.ShapeDtypeStruct(dims, F32)
    vm = lambda *dims: pltpu.VMEM(dims, BF16)
    vf = lambda *dims: pltpu.VMEM(dims, F32)
    up_grad, down_grad, gate_grad, total = pl.pallas_call(
        kernel,
        name="step",
        out_shape=(out(96, HID), out(HID, 96), out(2, 96, GATE), out(8, 128)),
        in_specs=[VMEM, SMEM, VMEM, VMEM, ANY, ANY, VMEM, VMEM, VMEM, ANY, VMEM, SMEM, SMEM],
        out_specs=(VMEM,) * 4,
        scratch_shapes=[
            vm(TOK, D),
            vm(D, TOK),
            vm(D, ROWS),
            vm(2, D, HID),
            vm(2, HID, D),
            vm(D, 2 * HID),
            vm(2, 4, NZ, 2, 48, 128),
            vm(D, 640),
            vm(2 * HID, 2 * GATE),
            vm(2 * GATE, 2 * HID),
            vm(TOK, 2 * HID),
            vm(2 * HID, TOK),
            vm(TOK, 2 * HID),
            vm(TOK, 2 * GATE),
            vm(TOK, 2 * GATE),
            vm(1024, D),
            vm(D, 1024),
            vm(TOK, 2 * HID),
            vm(TOK, 2 * GATE),
            vm(2 * HID, 2 * GATE),
            vm(640, 2 * HID),
            vf(256, HID),
            vm(4, 3, ROWS // 2, 2 * GATE),
            vm(4, 4, ROWS // 2, 2 * GATE),
            vf(NZ, 8, 128),
            vf(3, NZ, 8, 896),
            vf(3, 2, 8, 896),
            vf(NZ, 8, 128),
            vf(NZ, 128),
            vf(NZ, 128),
            vf(128, 128),
            vm(D, 2 * GATE),
            vm(8, 96, 2 * HID),
            vm(8, 96, 2 * HID),
            vm(D, GATE),
            vm(2, 4, 96, 2 * HID),
            vm(2, 4, 96, 2 * HID),
            vm(D, GATE),
            vm(2, 96, 2 * HID),
            vm(2, 2, 96, 2 * HID),
            vm(2, 48, HID),
            vm(2, 96, HID),
            vm(2, 2, 96, HID),
            vm(2, 4, 96, HID),
            vm(2, 48, HID),
            vm(2, 96, HID),
            vm(4, 3, 96, GATE),
            vm(4, 4, 96, GATE),
            vm(4, 192, GATE),
            vm(8, 96, GATE),
            vm(2, 96, GATE),
            vf(NZ, 8, 128),
            vf(4, 8, 128),
            vf(4, 8, 128),
            vf(2, 8, 128),
            pltpu.SemaphoreType.DMA((192,)),
            pltpu.SemaphoreType.DMA((192,)),
            pltpu.SemaphoreType.DMA((4,)),
        ],
        compiler_params=pltpu.CompilerParams(collective_id=1, has_side_effects=True, vmem_limit_bytes=VMEM_LIMIT),
    )(
        patch_class_features, live_tiles, tile_patient[None, :], ln_gain[None, :], up_weight, down_weight,
        tanh_weight, sigmoid_weight, score_weight[None, :], queue_keys, queue_labels[None, :], patient_labels,
        loss_scale.reshape(1),
    )
    return (up_grad, down_grad, gate_grad[0], gate_grad[1], total[:2].reshape(2 * 128), total[2, 0])


def solution(mesh):
    placed = (
        P(("pat", "tile"), None),
        P(("pat", "tile")),
        P(("pat", "tile")),
        P(),
        P(None, "tile"),
        P("tile", None),
        P("tile", None),
        P("tile", None),
        P(),
        P("tile", None),
        P("tile"),
        P("pat"),
        P(),
    )
    return jax.shard_map(
        per_device,
        mesh=mesh,
        in_specs=placed,
        out_specs=(P("pat", "tile"), P("tile", "pat"), P("tile", None), P("tile", None), P(), P()),
        check_vma=False,
    )
```

time: 1250 us -> 169 us (0.14)
  waiting for transfers between devices: 753 us -> 0 us
  blocking collectives: 399 us -> 0 us
  Pallas kernels: 0 us -> 157 us
  matrix products: 49.3 us -> 0 us
  other arithmetic: 23.6 us -> 0 us
  between operations: 17.4 us -> 1.94 us
    reduce_scatter x5 -> x0, waiting for transfers between devices: 516 us -> none  [the longest x1 204 us: per_device(): lax.psum_scatter(jnp.einsum('rd,rl->dl', head_in, sigmoid_pre, preferred_...]
    psum x5 -> x0, blocking collectives: 276 us -> none  [the longest x1 75.3 us: per_device(): lax.psum(jnp.dot(score_derivative_lines, direction_queue_entry, preferred...]
    all_gather x2 -> x0, waiting for transfers between devices: 236 us -> none  [the longest x1 121 us: per_device(): lax.all_gather(patch_class_features, 'tile', axis=0, tiled=True)]
    pallas_call x0 -> x1, Pallas kernels: none -> 157 us  [per_device(): pl.pallas_call(kernel, name='step', out_shape=(out(96, HID), out(HID, 96)...]
    all_gather x3 -> x0, blocking collectives: 123 us -> none  [the longest x1 44.6 us: per_device(): lax.all_gather(sigmoid_weight, 'tile', axis=0, tiled=True)]
    dot_general x14 -> x0, matrix products: 49.3 us -> none  [the longest x1 13.6 us: per_device(): jnp.einsum('rd,rf->df', normed, pre_grad, preferred_element_type=jnp.floa...]
  transfers between devices with their start and end apart: 7 -> 0, of which waited for: 7 -> 0; matrix products, arithmetic and copies ran while one was open for 2% -> 0% of each run, Pallas kernels for 0% -> 0%
where the time goes in v2:
time: 169 us; the launch traced here: 167 us
  Pallas kernels  157 us (93%)
  local copies, waits for them, and re-layouts  8.63 us (5%)
  between operations  1.94 us (1%)
    pallas_call x1, Pallas kernels, per_device(): pl.pallas_call(kernel, name='step', out_shape=(out(96, HID), out(HID, 96)...  157 us

profile of v2, /device:TPU:32, one launch (start us, length us, event | category | flops | bytes accessed | tf_op | source)
XLA Modules:
  0.0 167.4 jit_solution(7364774019127373037)
XLA Ops:
  1.3 1.3 broadcast_in_dim.13.gain
  3.2 156.9 %step.1 = (f32[96,384]{1,0:T(8,128)}, f32[384,96]{1,0:T(8,128)}, f32[2,96,256]{2,1,0:T(8,128)}, f32[8,128]{1,0:T(8,128)}) custom-call(bf16[128,1536]{1,0:T(8,128)(2,1)} %x_ref.1, s32[1]{0:T(128)S(6)} %copy.21.live, s32[1,128]{1,0:T(1,128)} %bitcast.14, f32[1,1536]{1,0:T(1,128)} %broadcast_in_dim.13.gain, bf16[1536,384]{1,0:T(8,128)(2,1)} %up_hbm.1, ...), custom_call_target="tpu_custom_call" | custom-call | tf_op jit(solution)/shard_map/step/pallas_call | solution.py:759
  160.1 1.7 %copy.19 = f32[384,96]{0,1:T(8,128)} copy(f32[384,96]{1,0:T(8,128)} %get-tuple-element.15) | data formatting | bytes 294912
  161.8 1.6 slice_bitcast_fusion
  163.4 1.2 slice_bitcast_fusion.2
  164.7 1.2 slice.15
  165.9 1.6 copy.23

commit v3 on v2

--- a/solution.py
+++ b/solution.py
@@ -227,7 +227,7 @@
     up_out, dn_out, gate_out, misc_out,
     n_all, n_t, x_t, up_b, dn_b, dn_t, wq, w_x, thru, thru_t, h_s, h_t, slope_s, part, uv_all, keys, keys_t,
     pg_s, pre_s, held_t, held, pre_t,
-    stage, recv, pbuf, zbuf, xbuf, sbuf, score_all, alpha_all, col_t,
+    stage, recv, pbuf, zbuf, xbuf, sbuf, score_all, alpha_all, pull_s,
     gt_p, up0, dn0, gt0, up_acc, dn_acc, g_acc, u_yh, u_yf, u_xh, u_xf, d_xh, d_xf, d_yh, d_yf,
     g_stage, g_recv, g_y, g_x, g_c, m_z, m_y, m_x, m_c,
     send_sem, recv_sem, local_sem,
@@ -258,20 +258,17 @@
     fetch_dn.start()
     fetch_keys.start()
 
-    def norm_rows(i, carry):
-        v = x_ref[pl.ds(pl.multiple_of(i * BLOCK16, BLOCK16), BLOCK16)].astype(F32)
+    def norm_rows(half):
+        v = x_ref[pl.ds(half * 64, 64)].astype(F32)
         center = v - jnp.mean(v, axis=1, keepdims=True)
         spread = jnp.mean(center * center, axis=1, keepdims=True)
-        n_all[pl.ds(pl.multiple_of(p.z * ROWS + i * BLOCK16, BLOCK16), BLOCK16)] = (
-            center * lax.rsqrt(spread + 1e-06) * gain[...]
-        ).astype(BF16)
-        return carry
+        n_all[rows_at(p.z, ROWS, half * 64, 64)] = (center * lax.rsqrt(spread + 1e-06) * gain[...][None, :]).astype(BF16)
 
     g_rows = pl.ds(pl.multiple_of(p.c * 48, 16), 48)
     g_lanes = lanes_at(lax.rem(p.y, 2), 128)
     wq[p.c, p.y, p.z, p.q] = jnp.where(p.y < 2, wt[g_rows, g_lanes], ws[g_rows, g_lanes])
 
-    lax.fori_loop(0, 4, norm_rows, 0)
+    norm_rows(0)
     pl.semaphore_wait(barrier, len(partners))
 
     tokens = ZGather(mail, p, n_all, ROWS)
@@ -279,16 +276,51 @@
     own_w = wq.at[p.c, p.y, p.z, p.q]
     mail.send(k_w, own_w, own_w, beside)
     tokens.step(0, (0, 1))
-    lax.fori_loop(4, 8, norm_rows, 0)
+    norm_rows(1)
     tokens.step(0, (2, 3))
 
-    k_half = mail.slots(2)
-    up_half = lambda q, c: up_b.at[q, rows_at(c, 768)]
-    dn_half = lambda q, c: dn_b.at[q, rows_at(c, 192)]
+    up_piece = lambda q, y, c: up_b.at[q, rows_at(y * 2 + c, 192)]
+    dn_piece = lambda q, y, c: dn_b.at[q, rows_at(y * 2 + c, 48)]
+    theirs, other = 1 - p.q, 1 - p.c
+    k_px, k_py, k_pm = mail.slots(2), mail.slots(6), mail.slots(8)
     fetch_up.wait()
-    mail.send(k_half, up_half(p.q, p.c), up_half(p.q, p.c), beside)
+    mail.send(k_px, up_piece(p.q, p.y, p.c), up_piece(p.q, p.y, p.c), beside)
     fetch_dn.wait()
-    mail.send(k_half + 1, dn_half(p.q, p.c), dn_half(p.q, p.c), beside)
+    mail.send(k_px + 1, dn_piece(p.q, p.y, p.c), dn_piece(p.q, p.y, p.c), beside)
+
+    def to_mate(d, piece, which):
+        mail.send(k_pm + which * 4 + d, piece(theirs, p.dy(d), p.c), piece(theirs, p.dy(d), p.c), mate)
+
+    def pieces_x():
+        for which, piece in enumerate((up_piece, dn_piece)):
+            block = piece(theirs, p.y, p.c)
+            mail.arrive(k_px + which, block, beside)
+            mail.send(k_py + which * 2, block, block, above)
+            mail.send(k_py + which * 2 + 1, block, block, below)
+            to_mate(0, piece, which)
+
+    def pieces_y():
+        for which, piece in enumerate((up_piece, dn_piece)):
+            under, over = piece(theirs, p.dy(-1), p.c), piece(theirs, p.dy(1), p.c)
+            mail.arrive(k_py + which * 2, under, below)
+            if which == 0:
+                mail.send(k_py + 4, under, under, above)
+            to_mate(3, piece, which)
+            mail.arrive(k_py + which * 2 + 1, over, above)
+            if which == 1:
+                mail.send(k_py + 5, over, over, below)
+            to_mate(1, piece, which)
+
+    def pieces_far():
+        mail.arrive(k_py + 4, up_piece(theirs, p.dy(2), p.c), below)
+        to_mate(2, up_piece, 0)
+        mail.arrive(k_py + 5, dn_piece(theirs, p.dy(2), p.c), above)
+        to_mate(2, dn_piece, 1)
+
+    def pieces_mate(which):
+        piece = (up_piece, dn_piece)[which]
+        for d in range(4):
+            mail.arrive(k_pm + which * 4 + d, piece(theirs, p.dy(d), other), mate)
 
     def hidden(owners, q):
         lhs = jnp.concatenate([n_all[rows_at(o, ROWS)] for o in owners], axis=0)
@@ -319,6 +351,18 @@
             if s < steps:
                 mail.send(key + s, block, block, z_dev(p.dz(way)))
 
+    def key_rows(i):
+        at = pl.ds(i * 256, 256)
+        v = keys[at].astype(F32)
+        keys[at] = (v * lax.rsqrt(jnp.sum(v * v, axis=1, keepdims=True) + 1e-06)).astype(BF16)
+
+    k_wy, k_wm = mail.slots(4), mail.slots(1)
+    w_y = lambda y: wq.at[p.c, y]
+    w_yh = lambda y, half: wq.at[p.c, y, pl.ds(half * 4, 4)]
+    near = [p.dz(1), p.dz(-1)]
+    mid = [p.dz(2), p.dz(-2)]
+    far = [p.dz(3), p.dz(-3)]
+
     mail.arrive(k_w, wq.at[p.c, p.y, p.z, 1 - p.q], beside)
     w_step(0)
     hidden([p.z], p.q)
@@ -326,59 +370,45 @@
     x_t[...] = x_ref[...].T
     w_step(1)
     tokens.step(1, (0, 1))
+    fetch_keys.wait()
+    key_rows(0)
+    pieces_x()
+    w_step(2)
     tokens.step(1, (2, 3))
-    w_step(2)
-    near = [p.dz(1), p.dz(-1)]
+    w_step(3)
     hidden(near, p.q)
     turn(near)
-    w_step(3)
-    fetch_keys.wait()
-
-    def key_rows(i, carry):
-        at = pl.ds(pl.multiple_of(i * BLOCK16, BLOCK16), BLOCK16)
-        v = keys[at].astype(F32)
-        keys[at] = (v * lax.rsqrt(jnp.sum(v * v, axis=1, keepdims=True) + 1e-06)).astype(BF16)
-        return carry
-
-    lax.fori_loop(0, 32, key_rows, 0)
+    key_rows(1)
     w_step(4)
-    k_wy = mail.slots(4)
-    w_y = lambda y: wq.at[p.c, y]
-    w_yh = lambda y, half: wq.at[p.c, y, pl.ds(half * 4, 4)]
     mail.send(k_wy, w_y(p.y), w_y(p.y), above)
     mail.send(k_wy + 1, w_y(p.y), w_y(p.y), below)
     tokens.step(2, (0, 1))
-    theirs, other = 1 - p.q, 1 - p.c
-    k_mate = mail.slots(3)
-    mail.arrive(k_half, up_half(theirs, p.c), beside)
-    mail.send(k_mate, up_half(theirs, p.c), up_half(theirs, p.c), mate)
+    pieces_y()
+    key_rows(2)
+    key_rows(3)
     tokens.step(2, (2, 3))
-    lax.fori_loop(32, 64, key_rows, 0)
-    mid = [p.dz(2), p.dz(-2)]
     hidden(mid, p.q)
     turn(mid)
     mail.arrive(k_wy, w_y(p.dy(-1)), below)
     mail.send(k_wy + 2, w_yh(p.dy(-1), 0), w_yh(p.dy(-1), 0), above)
     mail.arrive(k_wy + 1, w_y(p.dy(1)), above)
     mail.send(k_wy + 3, w_yh(p.dy(1), 1), w_yh(p.dy(1), 1), below)
-    mail.arrive(k_mate, up_half(theirs, other), mate)
-    hidden([p.z], theirs)
-    hidden(near, theirs)
+    pieces_far()
     tokens.step(3, (0, 1))
     mail.arrive(k_wy + 2, w_yh(p.dy(2), 0), below)
     mail.arrive(k_wy + 3, w_yh(p.dy(2), 1), above)
-    mail.send(k_mate + 2, wq.at[p.c], wq.at[p.c], mate)
-    tokens.step(3, (2, 3))
+    mail.send(k_wm, wq.at[p.c], wq.at[p.c], mate)
+    pieces_mate(0)
+    hidden([p.z], theirs)
+    hidden(near, theirs)
+    hidden(mid, theirs)
     for j in range(2):
         keys_t[:, pl.ds(j * 512, 512)] = keys[pl.ds(j * 512, 512)].T
-    hidden(mid, theirs)
-    far = [p.dz(3), p.dz(-3)]
+    tokens.step(3, (2, 3))
     hidden(far, p.q)
-    mail.arrive(k_half + 1, dn_half(theirs, p.c), beside)
-    mail.send(k_mate + 1, dn_half(theirs, p.c), dn_half(theirs, p.c), mate)
     hidden(far, theirs)
     turn(far)
-    mail.arrive(k_mate + 2, wq.at[other], mate)
+    mail.arrive(k_wm, wq.at[other], mate)
 
     def place_w(t, carry):
         for y in range(4):
@@ -389,7 +419,7 @@
 
     lax.fori_loop(0, 16, place_w, 0)
     w_full = lambda: w_x[:, pl.ds(0, 2 * GATE)]
-    mail.arrive(k_mate + 1, dn_half(theirs, other), mate)
+    pieces_mate(1)
     for q in range(2):
         thru[pl.ds(q * HID, HID)] = dot(dn_b[q], w_full()).astype(BF16)
 
@@ -461,6 +491,17 @@
     uv_all[own_rows, pl.ds(0, GATE)] = (common * (1.0 - tanh_val * tanh_val)).astype(BF16)
     uv_all[own_rows, pl.ds(GATE, GATE)] = (common * tanh_val * (1.0 - sigmoid_val)).astype(BF16)
     gather_uv.step(0)
+
+    def post(i, packed, small):
+        zbuf[i, p.z, :, pl.ds(0, 768)] = packed
+        zbuf[i, p.z, :, pl.ds(768, 128)] = small
+        swap_z[i].start()
+
+    def collect_z(i):
+        xbuf[i, p.q] = swap_z[i].total()
+        swap_x[i].start()
+
+    post(1, pack(label_sums), jnp.broadcast_to(positives, (8, 128)))
     vec_x = dot_two(mass, x_ref[...])
     swap_p.wait()
 
@@ -471,19 +512,11 @@
     mass_h = dot_two(mass_all, h_s[...])
     vec = dot_two(mass_h[:, :HID], dn_b[0]) + dot_two(mass_h[:, HID:], dn_b[1]) + vec_x
 
-    def post(i, packed, small):
-        zbuf[i, p.z, :, pl.ds(0, 768)] = packed
-        zbuf[i, p.z, :, pl.ds(768, 128)] = small
-        swap_z[i].start()
-
-    def collect_z(i):
-        xbuf[i, p.q] = swap_z[i].total()
-        swap_x[i].start()
-
     post(0, pack(vec), jnp.broadcast_to(total, (8, 128)))
+    collect_z(0)
     gather_uv.step(1)
-    collect_z(0)
-    post(1, pack(label_sums), jnp.broadcast_to(positives, (8, 128)))
+    collect_z(1)
+    thru_t[...] = thru[...].T
     summed = swap_x[0].total()
     total_mass = summed[:, 768:769]
     pooled = unpack(summed[:, :768]) / total_mass
@@ -495,30 +528,8 @@
     exp_part = jnp.sum(exps, axis=1, keepdims=True)
     pos_part = jnp.sum(same * logits, axis=1, keepdims=True)
     post(2, pack(dot_two(exps, keys[...])), jnp.where(lane == 0, exp_part, pos_part))
+    collect_z(2)
     gather_uv.step(2)
-    collect_z(1)
-    thru_t[...] = thru[...].T
-    gather_uv.step(3)
-    collect_z(2)
-    gather_uv.step(4)
-
-    def scaled(b, carry):
-        at = rows_at(b, ROWS)
-        pre_t[pl.ds(0, ROWS)] = dot(uv_all[at], thru_t[:, pl.ds(0, HID)])
-        pre_t[pl.ds(ROWS, ROWS)] = dot(uv_all[at], thru_t[:, pl.ds(HID, HID)])
-
-        def body(i, inner):
-            t = pl.multiple_of(i * BLOCK16, BLOCK16)
-            row = pl.ds(pl.multiple_of(b * ROWS + t, BLOCK16), BLOCK16)
-            for q in range(2):
-                lanes = pl.ds(q * HID, HID)
-                v = pre_t[pl.ds(pl.multiple_of(q * ROWS + t, BLOCK16), BLOCK16)]
-                pg_s[row, lanes] = (v * slope_s[row, lanes].astype(F32)).astype(BF16)
-            return inner
-
-        lax.fori_loop(0, ROWS // BLOCK16, body, 0)
-        return carry
-
     labels_total = swap_x[1].total()
     pos_count = labels_total[:, 768:769]
     queue_total = swap_x[2].total()
@@ -544,42 +555,42 @@
         block = jnp.where(first4, pbuf[z], 0.0)
         alpha_all[pl.ds(z, 1)] = jnp.sum(block / total_mass, axis=0, keepdims=True)
         score_all[pl.ds(z, 1)] = jnp.sum(jnp.where(block > 0.0, center, 0.0), axis=0, keepdims=True)
-    lax.fori_loop(0, NZ, scaled, 0)
+    gather_uv.step(3)
     pad = jnp.zeros((120, 768), F32)
     grad_h_pad = jnp.concatenate([jnp.where(first4_wide, grad_h, 0.0), pad], axis=0).astype(BF16)
+    rest = jnp.zeros((120, 128), F32)
+
+    def pulled(b, carry):
+        mass_b = jnp.where(first4, pbuf[b], 0.0)
+        weight = jnp.where(mass_b > 0.0, jnp.broadcast_to(alpha_all[pl.ds(b, 1)], (8, 128)), 0.0)
+        at = rows_at(b, ROWS)
+        turned = jnp.concatenate([weight, rest], axis=0).T.astype(BF16)
+        pull_s[at] = (dot(turned, grad_h_pad) * slope_s[at].astype(F32)).astype(BF16)
+        return carry + dot_two(weight, h_s[at])
+
+    held4 = lax.fori_loop(0, NZ, pulled, jnp.zeros((8, 768), F32))
+    held[pl.ds(512, 128)] = jnp.concatenate([jnp.where(first4_wide, held4, 0.0), pad], axis=0).astype(BF16)
     grad_pad = jnp.concatenate([pooled_grad, jnp.zeros((120, D), F32)], axis=0)
     for j in range(D // 128):
         w_x[pl.ds(j * 128, 128), pl.ds(512, 128)] = grad_pad[:, j * 128 : (j + 1) * 128].T.astype(BF16)
+    gather_uv.step(4)
+
+    def scaled(b, carry):
+        at = pl.ds(pl.multiple_of(b * 256, 256), 256)
+        pg_s[at] = (dot(uv_all[at], thru_t[...]) * slope_s[at].astype(F32)).astype(BF16)
+        return carry
+
+    lax.fori_loop(0, 4, scaled, 0)
     score_all[...] = alpha_all[...] * (swap_s.total() - score_all[...])
 
-    def columns(b, carry):
-        mass_b = jnp.where(first4, pbuf[b], 0.0)
-        weight = jnp.where(mass_b > 0.0, jnp.broadcast_to(alpha_all[pl.ds(b, 1)], (8, 128)), 0.0)
-        grad = jnp.broadcast_to(score_all[pl.ds(b, 1)], (8, 128))
-        turned = jnp.concatenate([weight, grad, jnp.zeros((112, 128), F32)], axis=0).T
-        col_t[...] = turned
+    def apply_scores(b, carry):
         at = rows_at(b, ROWS)
-        both = dot(turned.astype(BF16), grad_h_pad)
-        pre_t[pl.ds(0, ROWS)] = both[:, :HID]
-        pre_t[pl.ds(ROWS, ROWS)] = both[:, HID:]
-
-        def body(i, inner):
-            t = pl.multiple_of(i * BLOCK16, BLOCK16)
-            row = pl.ds(pl.multiple_of(b * ROWS + t, BLOCK16), BLOCK16)
-            s = col_t[pl.ds(t, BLOCK16)][:, 8:9]
-            pre_s[row] = (s * uv_all[row].astype(F32)).astype(BF16)
-            for q in range(2):
-                lanes = pl.ds(q * HID, HID)
-                v = pre_t[pl.ds(pl.multiple_of(q * ROWS + t, BLOCK16), BLOCK16)]
-                pg_s[row, lanes] = (
-                    s * pg_s[row, lanes].astype(F32) + v * slope_s[row, lanes].astype(F32)
-                ).astype(BF16)
-            return inner
-
-        lax.fori_loop(0, ROWS // BLOCK16, body, 0)
-        return carry + dot_two(weight, h_s[at])
-
-    held4 = lax.fori_loop(0, NZ, columns, jnp.zeros((8, 768), F32))
+        grad = jnp.broadcast_to(score_all[pl.ds(b, 1)], (ROWS, ROWS)).T[:, 0:1]
+        pre_s[at] = (grad * uv_all[at].astype(F32)).astype(BF16)
+        pg_s[at] = (grad * pg_s[at].astype(F32) + pull_s[at].astype(F32)).astype(BF16)
+        return carry
+
+    lax.fori_loop(0, NZ, apply_scores, 0)
     score_part = lax.dot_general(
         jnp.broadcast_to(score_all[pl.ds(p.z, 1)], (8, ROWS)), product, (((1,), (0,)), ((), ())),
         precision=HIGH, preferred_element_type=F32,
@@ -606,20 +617,20 @@
     misc_steps = misc_chain(misc)
     next(misc_steps)
 
-    for j in range(3):
-        held_t[pl.ds(j * 256, 256)] = dot(h_t[pl.ds(j * 256, 256)], pre_s[...]).astype(BF16)
-
-    def gate_rows(i, carry):
-        at = pl.ds(pl.multiple_of(i * 256, 256), 256)
-        gt_p[at] = (dot(dn_t[at], held_t[...]) + dot(x_t[at], pre_s[own_rows])).astype(BF16)
-        return carry
-
-    lax.fori_loop(0, 6, gate_rows, 0)
+    def gate_grads():
+        for j in range(3):
+            held_t[pl.ds(j * 256, 256)] = dot(h_t[pl.ds(j * 256, 256)], pre_s[...]).astype(BF16)
+
+        def gate_rows(i, carry):
+            at = pl.ds(pl.multiple_of(i * 512, 512), 512)
+            gt_p[at] = (dot(dn_t[at], held_t[...]) + dot(x_t[at], pre_s[own_rows])).astype(BF16)
+            return carry
+
+        lax.fori_loop(0, 3, gate_rows, 0)
+        mail.send(k_gt, gt_p.at[:, lanes_at(other, GATE)], gt0, mate)
+        held[pl.ds(0, 512)] = held_t[...].T
+
     k_gt = mail.slots(1)
-    mail.send(k_gt, gt_p.at[:, lanes_at(other, GATE)], gt0, mate)
-    held[pl.ds(0, 512)] = held_t[...].T
-    held[pl.ds(512, 128)] = jnp.concatenate([jnp.where(first4_wide, held4, 0.0), pad], axis=0).astype(BF16)
-
     up_p = lambda i, c: keys_t.at[pl.ds(pl.multiple_of((i * 2 + c) * 96, 96), 96), pl.ds(0, 768)]
     dn_p = lambda i, c: keys.at[
         pl.ds(pl.multiple_of((lax.rem(i, 4) * 2 + c) * 96, 96), 96), lanes_at(lax.div(i, 4), 768)
@@ -674,42 +685,6 @@
     k_x = mail.slots(3)
     in_c = Swap(mail, g_c, p.c, 2, c_dev)
 
-    up_go(0)
-    mail.arrive(k_gt, gt0, mate)
-    g_acc[...] = (gt_p[:, lanes_at(p.c, GATE)].astype(F32) + gt0[...].astype(F32)).astype(BF16)
-    zred.step(0)
-    up_go(1)
-    up_take(0)
-    step(up_y)
-    step(misc_steps)
-    zred.step(1)
-    up_go(2)
-    dn_go(0)
-    zred.step(2)
-    dn_go(1)
-    up_take(1)
-    up_take(2)
-    step(up_y)
-    dn_take(0)
-    dn_take(1)
-    step(dn_x)
-    zred.step(3)
-    step(misc_steps)
-    dn_go(2)
-    dn_go(3)
-    up_go(3)
-    g_y[p.y] = zred.total().astype(BF16)
-    in_y.start()
-    dn_take(2)
-    dn_take(3)
-    step(dn_x)
-    up_take(3)
-    step(misc_steps)
-    step(up_y)
-    add_into(up_acc.at[:, p.y], [u_yf.at[0], u_yf.at[1]])
-    step(up_x)
-    in_y.wait()
-
     def row_sum(q):
         rows = pl.ds(pl.multiple_of(q * 96, 96), 96)
         value = g_y[0, rows].astype(F32)
@@ -717,16 +692,55 @@
             value = value + g_y[j, rows].astype(F32)
         return value.astype(BF16)
 
+    up_go(0)
+    up_go(1)
+    gate_grads()
+    up_take(0)
+    step(up_y)
+    up_go(2)
+    dn_go(0)
+    mail.arrive(k_gt, gt0, mate)
+    g_acc[...] = (gt_p[:, lanes_at(p.c, GATE)].astype(F32) + gt0[...].astype(F32)).astype(BF16)
+    zred.step(0)
+    dn_go(1)
+    step(misc_steps)
+    up_take(1)
+    up_take(2)
+    step(up_y)
+    zred.step(1)
+    dn_take(0)
+    dn_take(1)
+    step(dn_x)
+    dn_go(2)
+    dn_go(3)
+    zred.step(2)
+    up_go(3)
+    step(misc_steps)
+    dn_take(2)
+    dn_take(3)
+    step(dn_x)
+    zred.step(3)
+    up_take(3)
+    step(up_y)
+    add_into(up_acc.at[:, p.y], [u_yf.at[0], u_yf.at[1]])
+    step(up_x)
+    g_y[p.y] = zred.total().astype(BF16)
+    in_y.start()
+    step(misc_steps)
+    step(dn_x)
+    add_into(dn_chunk_x(p.x), [d_xf.at[0], d_xf.at[1]])
+    step(dn_y)
+    step(up_x)
+    in_y.wait()
     for d in (1, 2, 3):
         there = p.dx(d)
         g_x[4 + d] = row_sum(lax.div(there, 2))
         mail.send(k_x + d - 1, g_x.at[4 + d], g_x.at[d], x_dev(there))
     g_x[0] = row_sum(p.q)
-    step(dn_x)
-    add_into(dn_chunk_x(p.x), [d_xf.at[0], d_xf.at[1]])
+    step(misc_steps)
     step(dn_y)
     step(up_x)
-    step(misc_steps)
+    up_out[...] = up_chunk(p.x)[...].astype(F32) + u_xf[0].astype(F32) + u_xf[1].astype(F32)
     for d in (1, 2, 3):
         mail.arrive(k_x + d - 1, g_x.at[d], x_dev(p.dx(-d)))
     value = g_x[0].astype(F32)
@@ -735,18 +749,25 @@
     g_c[p.c] = value.astype(BF16)
     in_c.start()
     step(dn_y)
-    step(up_x)
-    up_out[...] = up_chunk(p.x)[...].astype(F32) + u_xf[0].astype(F32) + u_xf[1].astype(F32)
+    dn_out[...] = dn_chunk(p.y)[...].astype(F32) + d_yf[0].astype(F32) + d_yf[1].astype(F32)
     in_c.wait()
     gate_out[...] = g_c[...].astype(F32)
-    step(dn_y)
-    dn_out[...] = (dn_chunk(p.y)[...].astype(F32) + d_yf[0].astype(F32) + d_yf[1].astype(F32)).T
     mail.finish()
 
 
 ANY = pl.BlockSpec(memory_space=pl.ANY)
 VMEM = pl.BlockSpec(memory_space=pltpu.VMEM)
 SMEM = pl.BlockSpec(memory_space=pltpu.SMEM)
+
+
+def hand_out(up, dn, gate, total, loss, up_out, dn_out, tanh_out, sigmoid_out, score_out, loss_out):
+    up_out[...] = up[...]
+    dn_out[...] = dn[...]
+    tanh_out[...] = gate[0]
+    sigmoid_out[...] = gate[1]
+    score_out[pl.ds(0, 128)] = total[0]
+    score_out[pl.ds(128, 128)] = total[1]
+    loss_out[0] = loss[2, 0]
 
 
 def per_device(
@@ -759,7 +780,7 @@
     up_grad, down_grad, gate_grad, total = pl.pallas_call(
         kernel,
         name="step",
-        out_shape=(out(96, HID), out(HID, 96), out(2, 96, GATE), out(8, 128)),
+        out_shape=(out(96, HID), out(96, HID), out(2, 96, GATE), out(8, 128)),
         in_specs=[VMEM, SMEM, VMEM, VMEM, ANY, ANY, VMEM, VMEM, VMEM, ANY, VMEM, SMEM, SMEM],
         out_specs=(VMEM,) * 4,
         scratch_shapes=[
@@ -793,7 +814,7 @@
             vf(NZ, 8, 128),
             vf(NZ, 128),
             vf(NZ, 128),
-            vf(128, 128),
+            vm(TOK, 2 * HID),
             vm(D, 2 * GATE),
             vm(8, 96, 2 * HID),
             vm(8, 96, 2 * HID),
@@ -824,11 +845,18 @@
         ],
         compiler_params=pltpu.CompilerParams(collective_id=1, has_side_effects=True, vmem_limit_bytes=VMEM_LIMIT),
     )(
-        patch_class_features, live_tiles, tile_patient[None, :], ln_gain[None, :], up_weight, down_weight,
+        patch_class_features, live_tiles, tile_patient[None, :], ln_gain, up_weight, down_weight,
         tanh_weight, sigmoid_weight, score_weight[None, :], queue_keys, queue_labels[None, :], patient_labels,
         loss_scale.reshape(1),
     )
-    return (up_grad, down_grad, gate_grad[0], gate_grad[1], total[:2].reshape(2 * 128), total[2, 0])
+    outputs = pl.pallas_call(
+        hand_out,
+        name="hand_out",
+        out_shape=(out(96, HID), out(96, HID), out(96, GATE), out(96, GATE), out(GATE), out(1)),
+        in_specs=[VMEM] * 4 + [SMEM],
+        out_specs=(VMEM,) * 5 + (SMEM,),
+    )(up_grad, down_grad, gate_grad, total, total)
+    return (outputs[0], outputs[1].T, *outputs[2:5], outputs[5].reshape(()))
 
 
 def solution(mesh):

time: 169 us -> 152 us (0.90)
  Pallas kernels: 157 us -> 147 us
  local copies, waits for them, and re-layouts: 8.63 us -> 0 us
    pallas_call x1 -> x2, Pallas kernels: 157 us -> 147 us  [the longest x1 146 us: per_device(): pl.pallas_call(kernel, name='step', out_shape=(out(96, HID), out(96, HID)...]
    unnamed x2 -> x0, local copies, waits for them, and re-layouts: 3.29 us -> none
where the time goes in v3:
time: 152 us; the launch traced here: 150 us
  Pallas kernels  147 us (97%)
  between operations  2.1 us (1%)
    pallas_call x1, Pallas kernels, per_device(): pl.pallas_call(kernel, name='step', out_shape=(out(96, HID), out(96, HID)...  146 us

profile of v3, /device:TPU:32, one launch (start us, length us, event | category | flops | bytes accessed | tf_op | source)
XLA Modules:
  0.0 149.5 jit_solution(5406478679065805503)
XLA Ops:
  1.9 145.5 %step.1 = (f32[96,384]{1,0:T(8,128)}, f32[96,384]{1,0:T(8,128)}, f32[2,96,256]{2,1,0:T(8,128)}, f32[8,128]{1,0:T(8,128)}) custom-call(bf16[128,1536]{1,0:T(8,128)(2,1)} %x_ref.1, s32[1]{0:T(128)S(6)} %copy.19.live, s32[1,128]{1,0:T(1,128)} %bitcast.9, f32[1536]{0:T(1024)} %gain.1, bf16[1536,384]{1,0:T(8,128)(2,1)} %up_hbm.1, bf16[384,1536]{1,0:T(8,128)(2,1)} %dn_hbm.1, ...), custom_call_target="tpu_custom_call" | custom-call | tf_op jit(solution)/shard_map/step/pallas_call | solution.py:780
  147.5 1.9 %hand_out.1 = (f32[96,384]{1,0:T(8,128)}, f32[96,384]{1,0:T(8,128)}, f32[96,256]{1,0:T(8,128)}, f32[96,256]{1,0:T(8,128)}, f32[256]{0:T(256)}, /*index=5*/f32[1]{0:T(128)}) custom-call(f32[96,384]{1,0:T(8,128)} %get-tuple-element.16.up, f32[96,384]{1,0:T(8,128)} %get-tuple-element.17.dn, f32[2,96,256]{2,1,0:T(8,128)} %get-tuple-element.18.gate, ...), custom_call_target="tpu_custom_call" | custom-call | tf_op jit(solution)/shard_map/hand_out/pallas_call | solution.py:852

commit v4 on v3

--- a/solution.py
+++ b/solution.py
@@ -127,9 +127,10 @@
     def piece(self, owner, half):
         return rows_at(owner, self.size, half * self.half, self.half)
 
-    def step(self, s):
+    def step(self, s, which=(0, 1, 2, 3)):
         p = self.place
-        for i, (way, half, steps) in enumerate(self.chains):
+        for i in which:
+            way, half, steps = self.chains[i]
             if s < steps:
                 dest = self.piece(p.dz(way * (steps - s)), half)
                 if s == 0:
@@ -225,11 +226,11 @@
 def kernel(
     x_ref, live, tile_patient, gain, up_hbm, dn_hbm, wt, ws, sw_ref, keys_hbm, qlab, plab, scale,
     up_out, dn_out, gate_out, misc_out,
-    n_all, n_t, x_t, up_b, dn_b, dn_t, wq, w_x, thru, thru_t, h_s, h_t, slope_s, part, uv_all, keys, keys_t,
-    pg_s, pre_s, held_t, held, pre_t,
+    n_all, n_t, x_t, x_mate, up_b, dn_b, dn_t, wq, w_x, w_c, thru, thru_t, h_s, h_t, slope_s, part, uv_all, keys, keys_t,
+    pg_s, pre_s, held_t, held_o, held_sum, held, pre2, gx, pre_t,
     stage, recv, pbuf, zbuf, xbuf, sbuf, score_all, alpha_all, pull_s,
-    gt_p, up0, dn0, gt0, up_acc, dn_acc, g_acc, u_yh, u_yf, u_xh, u_xf, d_xh, d_xf, d_yh, d_yf,
-    g_stage, g_recv, g_y, g_x, g_c, m_z, m_y, m_x, m_c,
+    up0, up_acc, dn_acc, g_acc, u_yh, u_yf, u_xh, u_xf, d_xh, d_xf, d_yh, d_yf,
+    g_stage, g_recv, g_t, g_y, g_x, g_c, m_z, m_y, m_x, m_c,
     send_sem, recv_sem, local_sem,
 ):
     p = Place()
@@ -266,18 +267,20 @@
 
     g_rows = pl.ds(pl.multiple_of(p.c * 48, 16), 48)
     g_lanes = lanes_at(lax.rem(p.y, 2), 128)
-    wq[p.c, p.y, p.z, p.q] = jnp.where(p.y < 2, wt[g_rows, g_lanes], ws[g_rows, g_lanes])
+    wq[p.c, p.y, p.q, p.z] = jnp.where(p.y < 2, wt[g_rows, g_lanes], ws[g_rows, g_lanes])
 
     norm_rows(0)
     pl.semaphore_wait(barrier, len(partners))
 
     tokens = ZGather(mail, p, n_all, ROWS)
-    k_w = mail.slots(1)
-    own_w = wq.at[p.c, p.y, p.z, p.q]
-    mail.send(k_w, own_w, own_w, beside)
+    k_wz, k_w = mail.slots(7), mail.slots(1)
+    w_z = lambda z: wq.at[p.c, p.y, p.q, z]
+    for d in range(1, NZ):
+        mail.send(k_wz + d - 1, w_z(p.z), w_z(p.z), z_dev(p.dz(d)))
     tokens.step(0, (0, 1))
     norm_rows(1)
-    tokens.step(0, (2, 3))
+    k_x0 = mail.slots(1)
+    mail.send(k_x0, x_ref, x_mate, mate)
 
     up_piece = lambda q, y, c: up_b.at[q, rows_at(y * 2 + c, 192)]
     dn_piece = lambda q, y, c: dn_b.at[q, rows_at(y * 2 + c, 48)]
@@ -340,17 +343,6 @@
         for o in owners:
             n_t[:, lanes_at(o, ROWS)] = n_all[rows_at(o, ROWS)].T
 
-    k_wz = mail.slots(7)
-    w_z = lambda z: wq.at[p.c, p.y, z]
-
-    def w_step(s):
-        for way, steps, key in ((1, 4, k_wz), (-1, 3, k_wz + 4)):
-            block = w_z(p.dz(-way * s))
-            if 0 < s <= steps:
-                mail.arrive(key + s - 1, block, z_dev(p.dz(-way)))
-            if s < steps:
-                mail.send(key + s, block, block, z_dev(p.dz(way)))
-
     def key_rows(i):
         at = pl.ds(i * 256, 256)
         v = keys[at].astype(F32)
@@ -358,49 +350,48 @@
 
     k_wy, k_wm = mail.slots(4), mail.slots(1)
     w_y = lambda y: wq.at[p.c, y]
-    w_yh = lambda y, half: wq.at[p.c, y, pl.ds(half * 4, 4)]
+    w_yh = lambda y, half: wq.at[p.c, y, half]
     near = [p.dz(1), p.dz(-1)]
     mid = [p.dz(2), p.dz(-2)]
     far = [p.dz(3), p.dz(-3)]
 
-    mail.arrive(k_w, wq.at[p.c, p.y, p.z, 1 - p.q], beside)
-    w_step(0)
     hidden([p.z], p.q)
     turn([p.z])
-    x_t[...] = x_ref[...].T
-    w_step(1)
-    tokens.step(1, (0, 1))
+    x_t[:, pl.ds(0, ROWS)] = x_ref[...].T
+    for d in range(1, NZ):
+        mail.arrive(k_wz + d - 1, w_z(p.dz(-d)), z_dev(p.dz(-d)))
+    mail.send(k_w, wq.at[p.c, p.y, p.q], wq.at[p.c, p.y, p.q], beside)
+    tokens.step(0, (2, 3))
     fetch_keys.wait()
     key_rows(0)
     pieces_x()
-    w_step(2)
+    mail.arrive(k_w, wq.at[p.c, p.y, theirs], beside)
+    mail.send(k_wy, w_y(p.y), w_y(p.y), above)
+    mail.send(k_wy + 1, w_y(p.y), w_y(p.y), below)
+    tokens.step(1, (0, 1))
+    key_rows(1)
     tokens.step(1, (2, 3))
-    w_step(3)
     hidden(near, p.q)
     turn(near)
-    key_rows(1)
-    w_step(4)
-    mail.send(k_wy, w_y(p.y), w_y(p.y), above)
-    mail.send(k_wy + 1, w_y(p.y), w_y(p.y), below)
+    key_rows(2)
+    pieces_y()
     tokens.step(2, (0, 1))
-    pieces_y()
-    key_rows(2)
     key_rows(3)
-    tokens.step(2, (2, 3))
-    hidden(mid, p.q)
-    turn(mid)
     mail.arrive(k_wy, w_y(p.dy(-1)), below)
     mail.send(k_wy + 2, w_yh(p.dy(-1), 0), w_yh(p.dy(-1), 0), above)
     mail.arrive(k_wy + 1, w_y(p.dy(1)), above)
     mail.send(k_wy + 3, w_yh(p.dy(1), 1), w_yh(p.dy(1), 1), below)
     pieces_far()
-    tokens.step(3, (0, 1))
+    tokens.step(2, (2, 3))
+    hidden(mid, p.q)
+    turn(mid)
     mail.arrive(k_wy + 2, w_yh(p.dy(2), 0), below)
     mail.arrive(k_wy + 3, w_yh(p.dy(2), 1), above)
     mail.send(k_wm, wq.at[p.c], wq.at[p.c], mate)
     pieces_mate(0)
     hidden([p.z], theirs)
     hidden(near, theirs)
+    tokens.step(3, (0, 1))
     hidden(mid, theirs)
     for j in range(2):
         keys_t[:, pl.ds(j * 512, 512)] = keys[pl.ds(j * 512, 512)].T
@@ -414,7 +405,7 @@
         for y in range(4):
             for c in range(2):
                 row = pl.multiple_of(t * 96 + c * 48, 16)
-                w_x[pl.ds(row, 48), pl.ds(y * 128, 128)] = wq[c, y, lax.div(t, 2), lax.rem(t, 2)]
+                w_x[pl.ds(row, 48), pl.ds(y * 128, 128)] = wq[c, y, lax.rem(t, 2), lax.div(t, 2)]
         return carry
 
     lax.fori_loop(0, 16, place_w, 0)
@@ -455,12 +446,13 @@
         rolled = pltpu.roll(v, 4, 0)
         return jnp.concatenate([jnp.where(first4_wide, v, rolled), jnp.where(first4_wide, rolled, v)], axis=1)
 
-    reduce.step(0)
+    reduce.step(0, (0, 1))
     turn([last])
-    for q in range(2):
-        dn_t[:, pl.ds(q * HID, HID)] = dn_b[q].T
+    dn_t[:, pl.ds(0, HID)] = dn_b[0].T
+    reduce.step(0, (2, 3))
+    dn_t[:, pl.ds(HID, HID)] = dn_b[1].T
     gate_x = dot(x_ref[...], w_full())
-    reduce.step(1)
+    reduce.step(1, (0, 1))
     same = jnp.zeros((8, 1024), jnp.int32)
     row_wide = lax.rem(lax.broadcasted_iota(jnp.int32, (8, 1024), 0), 4)
     labels = jnp.broadcast_to(qlab[...], (8, 1024))
@@ -469,10 +461,16 @@
     same = same.astype(F32)
     label_sums = dot(same.astype(BF16), keys[...])
     positives = jnp.sum(same, axis=1, keepdims=True)
-    reduce.step(2)
+    reduce.step(1, (2, 3))
     for z in range(NZ):
         h_t[:, pl.ds(z * ROWS, ROWS)] = h_s[pl.ds(z * ROWS, ROWS)].T
-    reduce.step(3)
+    reduce.step(2, (0, 1))
+    for i in range(8):
+        w_c[pl.ds(i * 96, 96), pl.ds(0, 512)] = w_x[pl.ds(pl.multiple_of((i * 2 + p.c) * 96, 96), 96), pl.ds(0, 512)]
+    reduce.step(2, (2, 3))
+    mail.arrive(k_x0, x_mate, mate)
+    x_t[:, pl.ds(ROWS, ROWS)] = x_mate[...].T
+    reduce.step(3, (0, 1))
     gates = reduce.total() + gate_x
     tanh_val = jnp.tanh(gates[:, :GATE])
     sigmoid_val = jax.nn.sigmoid(gates[:, GATE:])
@@ -541,7 +539,7 @@
     pooled_grad = (unit_grad - unit * jnp.sum(unit * unit_grad, axis=1, keepdims=True)) / length
 
     grad_h = dot_two(pooled_grad, dn_t[...])
-    own_dots = dot_two(pooled_grad, x_t[...])
+    own_dots = dot_two(pooled_grad, x_t[:, pl.ds(0, ROWS)])
     dots = dot_two(grad_h, h_t[...])
     for z in range(NZ):
         block = dots[:, z * ROWS : (z + 1) * ROWS] + jnp.where(p.z == z, own_dots, 0.0)
@@ -569,10 +567,10 @@
         return carry + dot_two(weight, h_s[at])
 
     held4 = lax.fori_loop(0, NZ, pulled, jnp.zeros((8, 768), F32))
-    held[pl.ds(512, 128)] = jnp.concatenate([jnp.where(first4_wide, held4, 0.0), pad], axis=0).astype(BF16)
-    grad_pad = jnp.concatenate([pooled_grad, jnp.zeros((120, D), F32)], axis=0)
-    for j in range(D // 128):
-        w_x[pl.ds(j * 128, 128), pl.ds(512, 128)] = grad_pad[:, j * 128 : (j + 1) * 128].T.astype(BF16)
+    k_g = mail.slots(1)
+    gx[0, :, pl.ds(0, D)] = pooled_grad
+    gx[0, :, pl.ds(D, 768)] = jnp.where(first4_wide, held4, 0.0)
+    mail.send(k_g, gx.at[0], gx.at[1], mate)
     gather_uv.step(4)
 
     def scaled(b, carry):
@@ -581,6 +579,15 @@
         return carry
 
     lax.fori_loop(0, 4, scaled, 0)
+    mail.arrive(k_g, gx.at[1], mate)
+    grad_pad = jnp.concatenate([gx[0, :, pl.ds(0, D)], gx[1, :, pl.ds(0, D)], jnp.zeros((112, D), F32)], axis=0)
+    for j in range(D // 128):
+        w_x[pl.ds(j * 128, 128), pl.ds(512, 128)] = grad_pad[:, j * 128 : (j + 1) * 128].T.astype(BF16)
+    for i in range(8):
+        w_c[pl.ds(i * 96, 96), pl.ds(512, 128)] = w_x[pl.ds(pl.multiple_of((i * 2 + p.c) * 96, 96), 96), pl.ds(512, 128)]
+    held[pl.ds(512, 128)] = jnp.concatenate(
+        [gx[0, :, pl.ds(D, 768)], gx[1, :, pl.ds(D, 768)], jnp.zeros((112, 768), F32)], axis=0
+    ).astype(BF16)
     score_all[...] = alpha_all[...] * (swap_s.total() - score_all[...])
 
     def apply_scores(b, carry):
@@ -617,25 +624,37 @@
     misc_steps = misc_chain(misc)
     next(misc_steps)
 
+    k_h, k_p = mail.slots(1), mail.slots(1)
+    for j in range(3):
+        held_t[pl.ds(j * 256, 256)] = dot(h_t[pl.ds(j * 256, 256)], pre_s[...]).astype(BF16)
+    mail.send(k_h, held_t, held_o, mate)
+    theirs_pre = pre_s.at[own_rows, lanes_at(other, GATE)]
+    mail.send(k_p, theirs_pre, pre2.at[pl.ds(ROWS, ROWS)], mate)
+    pre2[pl.ds(0, ROWS)] = pre_s[own_rows, lanes_at(p.c, GATE)]
+
+    def sum_held():
+        mail.arrive(k_h, held_o, mate)
+        total_held = (held_t[...].astype(F32) + held_o[...].astype(F32)).astype(BF16)
+        held_sum[...] = total_held
+        held[pl.ds(0, 512)] = total_held.T
+
     def gate_grads():
-        for j in range(3):
-            held_t[pl.ds(j * 256, 256)] = dot(h_t[pl.ds(j * 256, 256)], pre_s[...]).astype(BF16)
+        mail.arrive(k_p, pre2.at[pl.ds(ROWS, ROWS)], mate)
 
         def gate_rows(i, carry):
             at = pl.ds(pl.multiple_of(i * 512, 512), 512)
-            gt_p[at] = (dot(dn_t[at], held_t[...]) + dot(x_t[at], pre_s[own_rows])).astype(BF16)
+            g_acc[at] = (dot(dn_t[at], held_sum[:, lanes_at(p.c, GATE)]) + dot(x_t[at], pre2[...])).astype(BF16)
             return carry
 
         lax.fori_loop(0, 3, gate_rows, 0)
-        mail.send(k_gt, gt_p.at[:, lanes_at(other, GATE)], gt0, mate)
-        held[pl.ds(0, 512)] = held_t[...].T
-
-    k_gt = mail.slots(1)
+
+    def dn_rows(xl):
+        value = dot(w_c[rows_at(xl, 384)], held[...]).astype(BF16)
+        for y in range(4):
+            dn_acc[xl, y] = value[y * 96 : (y + 1) * 96]
+
     up_p = lambda i, c: keys_t.at[pl.ds(pl.multiple_of((i * 2 + c) * 96, 96), 96), pl.ds(0, 768)]
-    dn_p = lambda i, c: keys.at[
-        pl.ds(pl.multiple_of((lax.rem(i, 4) * 2 + c) * 96, 96), 96), lanes_at(lax.div(i, 4), 768)
-    ]
-    k_up0, k_dn0 = mail.slots(8), mail.slots(8)
+    k_up0 = mail.slots(8)
 
     def compute(block, lhs, rhs, index, k, buf):
         def body(j, carry):
@@ -661,11 +680,8 @@
         lax.fori_loop(0, 2, body, 0)
 
     up_index = [lambda j, d=d: j * 4 + p.dy(d) for d in (2, 1, -1, 0)]
-    dn_index = [lambda j, x=x, h=h: x * 4 + h * 2 + j for x in (p.xl, 1 - p.xl) for h in (0, 1)]
     up_go = lambda g: compute(up_p, n_t, pg_s, up_index[g], k_up0 + 2 * g, up0)
     up_take = lambda g: collect(up_p, up_index[g], k_up0 + 2 * g, up0, up_acc)
-    dn_go = lambda g: compute(dn_p, w_x, held, dn_index[g], k_dn0 + 2 * g, dn0)
-    dn_take = lambda g: collect(dn_p, dn_index[g], k_dn0 + 2 * g, dn0, dn_acc)
     rows_half = lambda ref, i: ref.at[pl.ds(i * 48, 48)]
     k_up, k_dn = mail.slots(8), mail.slots(8)
     up_chunk = lambda d: up_acc.at[lax.rem(d, 2), p.y, :, lanes_at(lax.div(d, 2), HID)]
@@ -685,73 +701,62 @@
     k_x = mail.slots(3)
     in_c = Swap(mail, g_c, p.c, 2, c_dev)
 
-    def row_sum(q):
-        rows = pl.ds(pl.multiple_of(q * 96, 96), 96)
-        value = g_y[0, rows].astype(F32)
-        for j in range(1, 4):
-            value = value + g_y[j, rows].astype(F32)
-        return value.astype(BF16)
-
     up_go(0)
+    sum_held()
+    gate_grads()
+    zred.step(0, (0, 1))
     up_go(1)
-    gate_grads()
+    zred.step(0, (2, 3))
+    dn_rows(p.xl)
+    dn_rows(1 - p.xl)
+    step(dn_x)
     up_take(0)
     step(up_y)
+    zred.step(1, (0, 1))
     up_go(2)
-    dn_go(0)
-    mail.arrive(k_gt, gt0, mate)
-    g_acc[...] = (gt_p[:, lanes_at(p.c, GATE)].astype(F32) + gt0[...].astype(F32)).astype(BF16)
-    zred.step(0)
-    dn_go(1)
+    zred.step(1, (2, 3))
+    up_go(3)
     step(misc_steps)
+    zred.step(2, (0, 1))
     up_take(1)
     up_take(2)
+    zred.step(2, (2, 3))
     step(up_y)
-    zred.step(1)
-    dn_take(0)
-    dn_take(1)
-    step(dn_x)
-    dn_go(2)
-    dn_go(3)
-    zred.step(2)
-    up_go(3)
-    step(misc_steps)
-    dn_take(2)
-    dn_take(3)
     step(dn_x)
     zred.step(3)
     up_take(3)
+    step(misc_steps)
+    sums = zred.total().astype(BF16)
+    g_t[0] = sums[:96]
+    g_t[1] = sums[96:]
+    for d in (1, 2, 3):
+        there = p.dx(d)
+        mail.send(k_x + d - 1, g_t.at[lax.div(there, 2)], g_x.at[d], x_dev(there))
     step(up_y)
     add_into(up_acc.at[:, p.y], [u_yf.at[0], u_yf.at[1]])
     step(up_x)
-    g_y[p.y] = zred.total().astype(BF16)
+    for d in (1, 2, 3):
+        mail.arrive(k_x + d - 1, g_x.at[d], x_dev(p.dx(-d)))
+    value = g_t[p.q].astype(F32)
+    for d in (1, 2, 3):
+        value = value + g_x[d].astype(F32)
+    g_y[p.y] = value.astype(BF16)
     in_y.start()
-    step(misc_steps)
     step(dn_x)
     add_into(dn_chunk_x(p.x), [d_xf.at[0], d_xf.at[1]])
     step(dn_y)
+    step(misc_steps)
+    g_c[p.c] = in_y.total().astype(BF16)
+    in_c.start()
     step(up_x)
-    in_y.wait()
-    for d in (1, 2, 3):
-        there = p.dx(d)
-        g_x[4 + d] = row_sum(lax.div(there, 2))
-        mail.send(k_x + d - 1, g_x.at[4 + d], g_x.at[d], x_dev(there))
-    g_x[0] = row_sum(p.q)
+    step(dn_y)
     step(misc_steps)
-    step(dn_y)
     step(up_x)
     up_out[...] = up_chunk(p.x)[...].astype(F32) + u_xf[0].astype(F32) + u_xf[1].astype(F32)
-    for d in (1, 2, 3):
-        mail.arrive(k_x + d - 1, g_x.at[d], x_dev(p.dx(-d)))
-    value = g_x[0].astype(F32)
-    for d in (1, 2, 3):
-        value = value + g_x[d].astype(F32)
-    g_c[p.c] = value.astype(BF16)
-    in_c.start()
+    in_c.wait()
+    gate_out[...] = g_c[...].astype(F32)
     step(dn_y)
     dn_out[...] = dn_chunk(p.y)[...].astype(F32) + d_yf[0].astype(F32) + d_yf[1].astype(F32)
-    in_c.wait()
-    gate_out[...] = g_c[...].astype(F32)
     mail.finish()
 
 
@@ -786,12 +791,14 @@
         scratch_shapes=[
             vm(TOK, D),
             vm(D, TOK),
-            vm(D, ROWS),
+            vm(D, 2 * ROWS),
+            vm(ROWS, D),
             vm(2, D, HID),
             vm(2, HID, D),
             vm(D, 2 * HID),
-            vm(2, 4, NZ, 2, 48, 128),
+            vm(2, 4, 2, NZ, 48, 128),
             vm(D, 640),
+            vm(768, 640),
             vm(2 * HID, 2 * GATE),
             vm(2 * GATE, 2 * HID),
             vm(TOK, 2 * HID),
@@ -804,7 +811,11 @@
             vm(TOK, 2 * HID),
             vm(TOK, 2 * GATE),
             vm(2 * HID, 2 * GATE),
+            vm(2 * HID, 2 * GATE),
+            vm(2 * HID, 2 * GATE),
             vm(640, 2 * HID),
+            vm(2 * ROWS, GATE),
+            vf(2, 8, D + 768),
             vf(256, HID),
             vm(4, 3, ROWS // 2, 2 * GATE),
             vm(4, 4, ROWS // 2, 2 * GATE),
@@ -815,10 +826,7 @@
             vf(NZ, 128),
             vf(NZ, 128),
             vm(TOK, 2 * HID),
-            vm(D, 2 * GATE),
             vm(8, 96, 2 * HID),
-            vm(8, 96, 2 * HID),
-            vm(D, GATE),
             vm(2, 4, 96, 2 * HID),
             vm(2, 4, 96, 2 * HID),
             vm(D, GATE),
@@ -832,8 +840,9 @@
             vm(2, 96, HID),
             vm(4, 3, 96, GATE),
             vm(4, 4, 96, GATE),
-            vm(4, 192, GATE),
-            vm(8, 96, GATE),
+            vm(2, 96, GATE),
+            vm(4, 96, GATE),
+            vm(4, 96, GATE),
             vm(2, 96, GATE),
             vf(NZ, 8, 128),
             vf(4, 8, 128),

time: 152 us -> 143 us (0.941); the launches traced: 150 us -> 143 us
  Pallas kernels: 147 us -> 141 us
    pallas_call x1, Pallas kernels: 146 us -> 139 us  [per_device(): pl.pallas_call(kernel, name='step', out_shape=(out(96, HID), out(96, HID)...]
where the time goes in v4:
time: 143 us
  Pallas kernels  141 us (99%)
  between operations  2.1 us (1%)
    pallas_call x1, Pallas kernels, per_device(): pl.pallas_call(kernel, name='step', out_shape=(out(96, HID), out(96, HID)...  139 us

profile of v4, /device:TPU:32, one launch (start us, length us, event | category | flops | bytes accessed | tf_op | source)
XLA Modules:
  0.0 143.2 jit_solution(11309180717575161500)
XLA Ops:
  1.9 139.2 %step.1 = (f32[96,384]{1,0:T(8,128)}, f32[96,384]{1,0:T(8,128)}, f32[2,96,256]{2,1,0:T(8,128)}, f32[8,128]{1,0:T(8,128)}) custom-call(bf16[128,1536]{1,0:T(8,128)(2,1)} %x_ref.1, s32[1]{0:T(128)S(6)} %copy.19.live, s32[1,128]{1,0:T(1,128)} %bitcast.9, f32[1536]{0:T(1024)} %gain.1, bf16[1536,384]{1,0:T(8,128)(2,1)} %up_hbm.1, bf16[384,1536]{1,0:T(8,128)(2,1)} %dn_hbm.1, ...), custom_call_target="tpu_custom_call" | custom-call | tf_op jit(solution)/shard_map/step/pallas_call | solution.py:785
  141.2 1.9 %hand_out.1 = (f32[96,384]{1,0:T(8,128)}, f32[96,384]{1,0:T(8,128)}, f32[96,256]{1,0:T(8,128)}, f32[96,256]{1,0:T(8,128)}, f32[256]{0:T(256)}, /*index=5*/f32[1]{0:T(128)}) custom-call(f32[96,384]{1,0:T(8,128)} %get-tuple-element.16.up, f32[96,384]{1,0:T(8,128)} %get-tuple-element.17.dn, f32[2,96,256]{2,1,0:T(8,128)} %get-tuple-element.18.gate, ...), custom_call_target="tpu_custom_call" | custom-call | tf_op jit(solution)/shard_map/hand_out/pallas_call | solution.py:861

commit v5 on v4

--- a/solution.py
+++ b/solution.py
@@ -302,23 +302,21 @@
             mail.send(k_py + which * 2 + 1, block, block, below)
             to_mate(0, piece, which)
 
+        for which, piece in enumerate((up_piece, dn_piece)):
+            block = piece(p.q, p.dy(2), p.c)
+            mail.send(k_py + 4 + which, block, block, beside)
+
     def pieces_y():
         for which, piece in enumerate((up_piece, dn_piece)):
-            under, over = piece(theirs, p.dy(-1), p.c), piece(theirs, p.dy(1), p.c)
-            mail.arrive(k_py + which * 2, under, below)
-            if which == 0:
-                mail.send(k_py + 4, under, under, above)
+            mail.arrive(k_py + which * 2, piece(theirs, p.dy(-1), p.c), below)
             to_mate(3, piece, which)
-            mail.arrive(k_py + which * 2 + 1, over, above)
-            if which == 1:
-                mail.send(k_py + 5, over, over, below)
+            mail.arrive(k_py + which * 2 + 1, piece(theirs, p.dy(1), p.c), above)
             to_mate(1, piece, which)
 
     def pieces_far():
-        mail.arrive(k_py + 4, up_piece(theirs, p.dy(2), p.c), below)
-        to_mate(2, up_piece, 0)
-        mail.arrive(k_py + 5, dn_piece(theirs, p.dy(2), p.c), above)
-        to_mate(2, dn_piece, 1)
+        for which, piece in enumerate((up_piece, dn_piece)):
+            mail.arrive(k_py + 4 + which, piece(theirs, p.dy(2), p.c), beside)
+            to_mate(2, piece, which)
 
     def pieces_mate(which):
         piece = (up_piece, dn_piece)[which]
@@ -364,41 +362,35 @@
     tokens.step(0, (2, 3))
     fetch_keys.wait()
     key_rows(0)
-    pieces_x()
+    tokens.step(1, (0, 1))
     mail.arrive(k_w, wq.at[p.c, p.y, theirs], beside)
     mail.send(k_wy, w_y(p.y), w_y(p.y), above)
     mail.send(k_wy + 1, w_y(p.y), w_y(p.y), below)
-    tokens.step(1, (0, 1))
-    key_rows(1)
+    pieces_x()
     tokens.step(1, (2, 3))
     hidden(near, p.q)
     turn(near)
+    key_rows(1)
+    tokens.step(2, (0, 1))
     key_rows(2)
-    pieces_y()
-    tokens.step(2, (0, 1))
     key_rows(3)
     mail.arrive(k_wy, w_y(p.dy(-1)), below)
     mail.send(k_wy + 2, w_yh(p.dy(-1), 0), w_yh(p.dy(-1), 0), above)
     mail.arrive(k_wy + 1, w_y(p.dy(1)), above)
     mail.send(k_wy + 3, w_yh(p.dy(1), 1), w_yh(p.dy(1), 1), below)
-    pieces_far()
     tokens.step(2, (2, 3))
     hidden(mid, p.q)
     turn(mid)
+    pieces_y()
     mail.arrive(k_wy + 2, w_yh(p.dy(2), 0), below)
     mail.arrive(k_wy + 3, w_yh(p.dy(2), 1), above)
     mail.send(k_wm, wq.at[p.c], wq.at[p.c], mate)
+    pieces_far()
+    tokens.step(3, (0, 1))
     pieces_mate(0)
     hidden([p.z], theirs)
     hidden(near, theirs)
-    tokens.step(3, (0, 1))
     hidden(mid, theirs)
-    for j in range(2):
-        keys_t[:, pl.ds(j * 512, 512)] = keys[pl.ds(j * 512, 512)].T
-    tokens.step(3, (2, 3))
-    hidden(far, p.q)
-    hidden(far, theirs)
-    turn(far)
     mail.arrive(k_wm, wq.at[other], mate)
 
     def place_w(t, carry):
@@ -419,6 +411,12 @@
         part[at] = dot(h_s[at], thru[...]).astype(BF16)
         return carry
 
+    tokens.step(3, (2, 3))
+    for j in range(2):
+        keys_t[:, pl.ds(j * 512, 512)] = keys[pl.ds(j * 512, 512)].T
+    hidden(far, p.q)
+    hidden(far, theirs)
+    turn(far)
     lax.fori_loop(0, NZ - 1, lambda d, carry: gate_part(lax.rem(p.z + 5 + d, NZ), carry), 0)
     tokens.step(4)
     last = p.dz(4)

time: 143 us -> 145 us (1.014)
  no operation moved by 1% of the time
where the time goes in v5:
time: 145 us
  Pallas kernels  142 us (98%)
  between operations  2.1 us (1%)
    pallas_call x1, Pallas kernels, per_device(): pl.pallas_call(kernel, name='step', out_shape=(out(96, HID), out(96, HID)...  141 us

profile of v5, /device:TPU:32, one launch (start us, length us, event | category | flops | bytes accessed | tf_op | source)
XLA Modules:
  0.0 144.5 jit_solution(2899234875487913113)
XLA Ops:
  1.9 140.6 %step.1 = (f32[96,384]{1,0:T(8,128)}, f32[96,384]{1,0:T(8,128)}, f32[2,96,256]{2,1,0:T(8,128)}, f32[8,128]{1,0:T(8,128)}) custom-call(bf16[128,1536]{1,0:T(8,128)(2,1)} %x_ref.1, s32[1]{0:T(128)S(6)} %copy.19.live, s32[1,128]{1,0:T(1,128)} %bitcast.9, f32[1536]{0:T(1024)} %gain.1, bf16[1536,384]{1,0:T(8,128)(2,1)} %up_hbm.1, bf16[384,1536]{1,0:T(8,128)(2,1)} %dn_hbm.1, ...), custom_call_target="tpu_custom_call" | custom-call | tf_op jit(solution)/shard_map/step/pallas_call | solution.py:783
  142.5 1.9 %hand_out.1 = (f32[96,384]{1,0:T(8,128)}, f32[96,384]{1,0:T(8,128)}, f32[96,256]{1,0:T(8,128)}, f32[96,256]{1,0:T(8,128)}, f32[256]{0:T(256)}, /*index=5*/f32[1]{0:T(128)}) custom-call(f32[96,384]{1,0:T(8,128)} %get-tuple-element.16.up, f32[96,384]{1,0:T(8,128)} %get-tuple-element.17.dn, f32[2,96,256]{2,1,0:T(8,128)} %get-tuple-element.18.gate, ...), custom_call_target="tpu_custom_call" | custom-call | tf_op jit(solution)/shard_map/hand_out/pallas_call | solution.py:859

commit v6 on v5

--- a/solution.py
+++ b/solution.py
@@ -81,9 +81,11 @@
             device_id=device, device_id_type=MESH,
         ).wait_recv()
 
-    def finish(self):
-        for copy in self.sent:
+    def settle(self, keep=0):
+        done = len(self.sent) - keep
+        for copy in self.sent[:done]:
             copy.wait_send()
+        self.sent = self.sent[done:]
 
 
 def rows_at(index, size, offset=0, count=None):
@@ -228,7 +230,7 @@
     up_out, dn_out, gate_out, misc_out,
     n_all, n_t, x_t, x_mate, up_b, dn_b, dn_t, wq, w_x, w_c, thru, thru_t, h_s, h_t, slope_s, part, uv_all, keys, keys_t,
     pg_s, pre_s, held_t, held_o, held_sum, held, pre2, gx, pre_t,
-    stage, recv, pbuf, zbuf, xbuf, sbuf, score_all, alpha_all, pull_s,
+    stage, recv, pbuf, vbuf, zbuf, xbuf, sbuf, score_all, alpha_all, pull_s,
     up0, up_acc, dn_acc, g_acc, u_yh, u_yf, u_xh, u_xf, d_xh, d_xf, d_yh, d_yf,
     g_stage, g_recv, g_t, g_y, g_x, g_c, m_z, m_y, m_x, m_c,
     send_sem, recv_sem, local_sem,
@@ -427,7 +429,7 @@
     reduce = ZReduce(mail, p, part, ROWS, stage, recv)
     gather_uv = ZGather(mail, p, uv_all, ROWS)
     swap_p = Swap(mail, pbuf, p.z, NZ, z_dev)
-    swap_z = [Swap(mail, zbuf.at[i], p.z, NZ, z_dev) for i in range(3)]
+    swap_z = [Swap(mail, ref, p.z, NZ, z_dev) for ref in (vbuf, zbuf.at[0], zbuf.at[1])]
     swap_x = [Swap(mail, xbuf.at[i], p.q, 2, q_dev) for i in range(3)]
     swap_s = Swap(mail, sbuf, p.z, NZ, z_dev)
 
@@ -469,6 +471,7 @@
     mail.arrive(k_x0, x_mate, mate)
     x_t[:, pl.ds(ROWS, ROWS)] = x_mate[...].T
     reduce.step(3, (0, 1))
+    mail.settle(20)
     gates = reduce.total() + gate_x
     tanh_val = jnp.tanh(gates[:, :GATE])
     sigmoid_val = jax.nn.sigmoid(gates[:, GATE:])
@@ -489,8 +492,8 @@
     gather_uv.step(0)
 
     def post(i, packed, small):
-        zbuf[i, p.z, :, pl.ds(0, 768)] = packed
-        zbuf[i, p.z, :, pl.ds(768, 128)] = small
+        zbuf[i - 1, p.z, :, pl.ds(0, 768)] = packed
+        zbuf[i - 1, p.z, :, pl.ds(768, 128)] = small
         swap_z[i].start()
 
     def collect_z(i):
@@ -508,8 +511,17 @@
     mass_h = dot_two(mass_all, h_s[...])
     vec = dot_two(mass_h[:, :HID], dn_b[0]) + dot_two(mass_h[:, HID:], dn_b[1]) + vec_x
 
-    post(0, pack(vec), jnp.broadcast_to(total, (8, 128)))
-    collect_z(0)
+    packed = pack(vec)
+    top = total.astype(BF16).astype(F32)
+    small = jnp.where(lane == 0, top, total - top)
+    vbuf[p.z, :, pl.ds(0, 384)] = jnp.concatenate([packed[:, :384], packed[:, 384:]], axis=0).astype(BF16)
+    vbuf[p.z, :, pl.ds(384, 128)] = jnp.concatenate([small, small], axis=0).astype(BF16)
+    swap_z[0].start()
+    both = swap_z[0].total()
+    xbuf[0, p.q, :, pl.ds(0, 384)] = both[:8, :384]
+    xbuf[0, p.q, :, pl.ds(384, 384)] = both[8:, :384]
+    xbuf[0, p.q, :, pl.ds(768, 128)] = jnp.broadcast_to(both[:8, 384:385] + both[:8, 385:386], (8, 128))
+    swap_x[0].start()
     gather_uv.step(1)
     collect_z(1)
     thru_t[...] = thru[...].T
@@ -586,6 +598,7 @@
     held[pl.ds(512, 128)] = jnp.concatenate(
         [gx[0, :, pl.ds(D, 768)], gx[1, :, pl.ds(D, 768)], jnp.zeros((112, 768), F32)], axis=0
     ).astype(BF16)
+    mail.settle(12)
     score_all[...] = alpha_all[...] * (swap_s.total() - score_all[...])
 
     def apply_scores(b, carry):
@@ -749,13 +762,14 @@
     step(up_x)
     step(dn_y)
     step(misc_steps)
+    mail.settle(8)
     step(up_x)
     up_out[...] = up_chunk(p.x)[...].astype(F32) + u_xf[0].astype(F32) + u_xf[1].astype(F32)
     in_c.wait()
     gate_out[...] = g_c[...].astype(F32)
     step(dn_y)
     dn_out[...] = dn_chunk(p.y)[...].astype(F32) + d_yf[0].astype(F32) + d_yf[1].astype(F32)
-    mail.finish()
+    mail.settle()
 
 
 ANY = pl.BlockSpec(memory_space=pl.ANY)
@@ -818,7 +832,8 @@
             vm(4, 3, ROWS // 2, 2 * GATE),
             vm(4, 4, ROWS // 2, 2 * GATE),
             vf(NZ, 8, 128),
-            vf(3, NZ, 8, 896),
+            vm(NZ, 16, 512),
+            vf(2, NZ, 8, 896),
             vf(3, 2, 8, 896),
             vf(NZ, 8, 128),
             vf(NZ, 128),

time: 145 us -> 143 us (0.986)
    pallas_call x1, Pallas kernels: 141 us -> 139 us  [per_device(): pl.pallas_call(kernel, name='step', out_shape=(out(96, HID), out(96, HID)...]
where the time goes in v6:
time: 143 us
  Pallas kernels  141 us (99%)
  between operations  2.1 us (1%)
    pallas_call x1, Pallas kernels, per_device(): pl.pallas_call(kernel, name='step', out_shape=(out(96, HID), out(96, HID)...  139 us

profile of v6, /device:TPU:32, one launch (start us, length us, event | category | flops | bytes accessed | tf_op | source)
XLA Modules:
  0.0 142.7 jit_solution(4697296247090700906)
XLA Ops:
  1.9 138.7 %step.1 = (f32[96,384]{1,0:T(8,128)}, f32[96,384]{1,0:T(8,128)}, f32[2,96,256]{2,1,0:T(8,128)}, f32[8,128]{1,0:T(8,128)}) custom-call(bf16[128,1536]{1,0:T(8,128)(2,1)} %x_ref.1, s32[1]{0:T(128)S(6)} %copy.19.live, s32[1,128]{1,0:T(1,128)} %bitcast.9, f32[1536]{0:T(1024)} %gain.1, bf16[1536,384]{1,0:T(8,128)(2,1)} %up_hbm.1, bf16[384,1536]{1,0:T(8,128)(2,1)} %dn_hbm.1, ...), custom_call_target="tpu_custom_call" | custom-call | tf_op jit(solution)/shard_map/step/pallas_call | solution.py:797
  140.7 1.9 %hand_out.1 = (f32[96,384]{1,0:T(8,128)}, f32[96,384]{1,0:T(8,128)}, f32[96,256]{1,0:T(8,128)}, f32[96,256]{1,0:T(8,128)}, f32[256]{0:T(256)}, /*index=5*/f32[1]{0:T(128)}) custom-call(f32[96,384]{1,0:T(8,128)} %get-tuple-element.16.up, f32[96,384]{1,0:T(8,128)} %get-tuple-element.17.dn, f32[2,96,256]{2,1,0:T(8,128)} %get-tuple-element.18.gate, ...), custom_call_target="tpu_custom_call" | custom-call | tf_op jit(solution)/shard_map/hand_out/pallas_call | solution.py:874

commit v7 on v6

--- a/solution.py
+++ b/solution.py
@@ -635,19 +635,21 @@
     misc_steps = misc_chain(misc)
     next(misc_steps)
 
-    k_h, k_p = mail.slots(1), mail.slots(1)
+    k_h, k_p = mail.slots(2), mail.slots(1)
     for j in range(3):
         held_t[pl.ds(j * 256, 256)] = dot(h_t[pl.ds(j * 256, 256)], pre_s[...]).astype(BF16)
-    mail.send(k_h, held_t, held_o, mate)
+    half_of = lambda ref, c: ref.at[:, lanes_at(c, GATE)]
+    mail.send(k_h, half_of(held_t, other), half_of(held_o, other), mate)
     theirs_pre = pre_s.at[own_rows, lanes_at(other, GATE)]
     mail.send(k_p, theirs_pre, pre2.at[pl.ds(ROWS, ROWS)], mate)
     pre2[pl.ds(0, ROWS)] = pre_s[own_rows, lanes_at(p.c, GATE)]
 
-    def sum_held():
-        mail.arrive(k_h, held_o, mate)
-        total_held = (held_t[...].astype(F32) + held_o[...].astype(F32)).astype(BF16)
-        held_sum[...] = total_held
-        held[pl.ds(0, 512)] = total_held.T
+    def sum_held(k, c):
+        mail.arrive(k, half_of(held_o, c), mate)
+        lanes = lanes_at(c, GATE)
+        total_held = (held_t[:, lanes].astype(F32) + held_o[:, lanes].astype(F32)).astype(BF16)
+        held_sum[:, lanes] = total_held
+        held[rows_at(c, GATE)] = total_held.T
 
     def gate_grads():
         mail.arrive(k_p, pre2.at[pl.ds(ROWS, ROWS)], mate)
@@ -713,11 +715,13 @@
     in_c = Swap(mail, g_c, p.c, 2, c_dev)
 
     up_go(0)
-    sum_held()
+    mail.send(k_h + 1, half_of(held_t, p.c), half_of(held_o, p.c), mate)
+    sum_held(k_h, p.c)
     gate_grads()
     zred.step(0, (0, 1))
     up_go(1)
     zred.step(0, (2, 3))
+    sum_held(k_h + 1, other)
     dn_rows(p.xl)
     dn_rows(1 - p.xl)
     step(dn_x)

time: 143 us -> 142 us (level)
  no operation moved by 1% of the time
where the time goes in v7:
time: 142 us
  Pallas kernels  140 us (99%)
  between operations  2.1 us (1%)
    pallas_call x1, Pallas kernels, per_device(): pl.pallas_call(kernel, name='step', out_shape=(out(96, HID), out(96, HID)...  138 us

profile of v7, /device:TPU:32, one launch (start us, length us, event | category | flops | bytes accessed | tf_op | source)
XLA Modules:
  0.0 141.9 jit_solution(9765706819976794090)
XLA Ops:
  1.9 137.9 %step.1 = (f32[96,384]{1,0:T(8,128)}, f32[96,384]{1,0:T(8,128)}, f32[2,96,256]{2,1,0:T(8,128)}, f32[8,128]{1,0:T(8,128)}) custom-call(bf16[128,1536]{1,0:T(8,128)(2,1)} %x_ref.1, s32[1]{0:T(128)S(6)} %copy.19.live, s32[1,128]{1,0:T(1,128)} %bitcast.9, f32[1536]{0:T(1024)} %gain.1, bf16[1536,384]{1,0:T(8,128)(2,1)} %up_hbm.1, bf16[384,1536]{1,0:T(8,128)(2,1)} %dn_hbm.1, ...), custom_call_target="tpu_custom_call" | custom-call | tf_op jit(solution)/shard_map/step/pallas_call | solution.py:801
  139.9 1.9 %hand_out.1 = (f32[96,384]{1,0:T(8,128)}, f32[96,384]{1,0:T(8,128)}, f32[96,256]{1,0:T(8,128)}, f32[96,256]{1,0:T(8,128)}, f32[256]{0:T(256)}, /*index=5*/f32[1]{0:T(128)}) custom-call(f32[96,384]{1,0:T(8,128)} %get-tuple-element.16.up, f32[96,384]{1,0:T(8,128)} %get-tuple-element.17.dn, f32[2,96,256]{2,1,0:T(8,128)} %get-tuple-element.18.gate, ...), custom_call_target="tpu_custom_call" | custom-call | tf_op jit(solution)/shard_map/hand_out/pallas_call | solution.py:878
